TPU v7x, 128 devices: a whole 4x4x4 slice. The times are simulated.
128 devices in a mesh: var: 8 (over z_lo, y), lon: 16 (over x, z_hi, core).
Axes of the slice: x: 4, y: 4, z: 4 (z_hi: 2, z_lo: 2; z = z_hi * 2 + z_lo), core: 2. Of those that a mesh axis runs over, the one named last changes fastest.
Arguments:
- pixels: bfloat16 [8, 5, 16, 16384], P('var', None, None, 'lon'), may hold values from -6 to 6
- w_embed: bfloat16 [80, 512], replicated, may hold values from -0.625 to 0.625
- level_embed: bfloat16 [8, 512], replicated, may hold values from -6 to 6
- latents: bfloat16 [3, 512], replicated, may hold values from -96 to 96
- w_query: bfloat16 [512, 1024], replicated, may hold values from -0.25 to 0.25
- w_key: bfloat16 [512, 1024], replicated, may hold values from -0.25 to 0.25
- w_value: bfloat16 [512, 1024], replicated, may hold values from -0.25 to 0.25
- w_out: bfloat16 [1024, 512], replicated, may hold values from -0.1875 to 0.1875
- w_up: bfloat16 [512, 2048], replicated, may hold values from -0.25 to 0.25
- w_down: bfloat16 [2048, 512], replicated, may hold values from -0.125 to 0.125
- cotangent: bfloat16 [3, 16384, 512], P(None, ('lon', 'var')), may hold values from -0.02734375 to 0.02734375
Outputs:
- pooled: bfloat16 [3, 16384, 512], P(None, ('lon', 'var'))
- grad_embed: float32 [80, 512], replicated
- grad_level: float32 [8, 512], replicated
- grad_latents: float32 [3, 512], replicated
- grad_query: float32 [512, 1024], replicated
- grad_key: float32 [512, 1024], replicated
- grad_value: float32 [512, 1024], replicated
- grad_out: float32 [1024, 512], replicated
- grad_up: float32 [512, 2048], P(None, 'lon')
- grad_down: float32 [2048, 512], P('lon')
All inputs are finite; a program needn't handle non-finite values.
Results may differ from a plain program's by a relative error of at most 0.024.
The roundings to bfloat16 on the way count: a program that leaves them out, or rounds other values in their place, can miss the bound.
Values may be sent and summed in bfloat16 or wider, within the bound.
A program may use at most 128 MiB of HBM per device.

v0:
```python
import math

import jax
import jax.numpy as jnp
from jax import lax
from jax.sharding import PartitionSpec as P

HEADS = 16


F32 = jnp.float32
BF16 = jnp.bfloat16
EPSILON = 1e-05


def contract(form, left, right):
    return jnp.einsum(form, left, right, preferred_element_type=F32)


def flat_outer(left, right):
    left_rows = left.reshape(-1, left.shape[-1])
    right_rows = right.reshape(-1, right.shape[-1])
    return lax.dot_general(
        left_rows, right_rows, (((0,), (0,)), ((), ())), preferred_element_type=F32
    )


def times_transposed(left, weight):
    return lax.dot_general(
        left, weight, (((left.ndim - 1,), (1,)), ((), ())), preferred_element_type=F32
    )


def embed_levels(pixels, w_embed, level_rows):
    levels, variables, pixel_count, patches = pixels.shape
    folded = pixels.reshape(levels, variables * pixel_count, patches)
    summed = lax.dot_general(folded, w_embed, (((1,), (0,)), ((), ())), preferred_element_type=F32)
    return (summed + level_rows.astype(F32)[:, None, :]).astype(BF16)


def embed_grads(pixels, d_tokens):
    levels, variables, pixel_count, patches = pixels.shape
    folded = pixels.reshape(levels, variables * pixel_count, patches)
    grad_embed = lax.dot_general(
        folded, d_tokens, (((0, 2), (0, 1)), ((), ())), preferred_element_type=F32
    )
    return (grad_embed, jnp.sum(d_tokens.astype(F32), axis=1))


def front(tokens, latents, w_query, w_key, w_value, w_out, w_up, w_down, cotangent):
    levels, patches, width = tokens.shape
    n_lat = latents.shape[0]
    inner = w_key.shape[1]
    head_dim = inner // HEADS
    scale = 1.0 / math.sqrt(head_dim)
    whole = tokens.astype(F32)
    center = whole - jnp.mean(whole, axis=-1, keepdims=True)
    inverse = lax.rsqrt(jnp.mean(center * center, axis=-1, keepdims=True) + EPSILON)
    unit = center * inverse
    normed = unit.astype(BF16)
    keys = jnp.dot(normed, w_key, preferred_element_type=F32).astype(BF16)
    values = jnp.dot(normed, w_value, preferred_element_type=F32).astype(BF16)
    queries = jnp.dot(latents, w_query, preferred_element_type=F32).astype(BF16)
    key_heads = keys.reshape(levels, patches, HEADS, head_dim)
    value_heads = values.reshape(levels, patches, HEADS, head_dim)
    query_heads = queries.reshape(n_lat, HEADS, head_dim)
    scores = contract("qhj,lphj->hqlp", query_heads, key_heads) * scale
    highest = jnp.max(scores, axis=2, keepdims=True)
    expo = jnp.exp(scores - highest)
    probs = expo / jnp.sum(expo, axis=2, keepdims=True)
    weights = probs.astype(BF16)
    mixed = (
        contract("hqlp,lphj->qphj", weights, value_heads)
        .astype(BF16)
        .reshape(n_lat, patches, inner)
    )
    attended = (
        latents.astype(F32)[:, None, :] + jnp.dot(mixed, w_out, preferred_element_type=F32)
    ).astype(BF16)
    pre_act = jnp.dot(attended, w_up, preferred_element_type=F32)
    hidden = jax.nn.gelu(pre_act).astype(BF16)
    pooled = (attended.astype(F32) + jnp.dot(hidden, w_down, preferred_element_type=F32)).astype(
        BF16
    )
    grad_down = flat_outer(hidden, cotangent)
    d_hidden = times_transposed(cotangent, w_down)
    d_pre = jax.vjp(jax.nn.gelu, pre_act)[1](d_hidden)[0].astype(BF16)
    grad_up_rows = flat_outer(d_pre, attended)
    d_att = cotangent.astype(F32) + times_transposed(d_pre, w_up)
    d_att_b = d_att.astype(BF16)
    grad_out = flat_outer(mixed, d_att_b)
    saved = (
        unit,
        inverse,
        normed,
        key_heads,
        value_heads,
        query_heads,
        probs,
        weights,
        d_att,
        d_att_b,
    )
    return (pooled, (grad_out, grad_up_rows, grad_down), saved)


def back(saved, latents, w_query, w_key, w_value, w_out):
    unit, inverse, normed, key_heads, value_heads, query_heads, probs, weights, d_att, d_att_b = (
        saved
    )
    levels, patches, heads, head_dim = key_heads.shape
    n_lat = query_heads.shape[0]
    inner = heads * head_dim
    scale = 1.0 / math.sqrt(head_dim)
    d_mixed = times_transposed(d_att_b, w_out).astype(BF16).reshape(n_lat, patches, heads, head_dim)
    d_weights = contract("qphj,lphj->hqlp", d_mixed, value_heads)
    d_values = (
        contract("hqlp,qphj->lphj", weights, d_mixed).astype(BF16).reshape(levels, patches, inner)
    )
    d_scores = (
        probs * (d_weights - jnp.sum(probs * d_weights, axis=2, keepdims=True)) * scale
    ).astype(BF16)
    d_queries = contract("hqlp,lphj->qhj", d_scores, key_heads).reshape(n_lat, inner)
    d_keys = (
        contract("hqlp,qhj->lphj", d_scores, query_heads)
        .astype(BF16)
        .reshape(levels, patches, inner)
    )
    grad_key = flat_outer(normed, d_keys)
    grad_value = flat_outer(normed, d_values)
    d_normed = times_transposed(d_keys, w_key) + times_transposed(d_values, w_value)
    d_tokens = (
        inverse
        * (
            d_normed
            - jnp.mean(d_normed, axis=-1, keepdims=True)
            - unit * jnp.mean(d_normed * unit, axis=-1, keepdims=True)
        )
    ).astype(BF16)
    grad_query = lax.dot_general(
        latents.astype(F32), d_queries, (((0,), (0,)), ((), ())), precision=lax.Precision.HIGHEST
    )
    grad_lat = jnp.sum(d_att, axis=1) + lax.dot_general(
        d_queries, w_query.astype(F32), (((1,), (1,)), ((), ())), precision=lax.Precision.HIGHEST
    )
    return (d_tokens, (grad_query, grad_key, grad_value, grad_lat))


def ffn_sums(grad_up_rows, grad_down):
    up_part, down_part = (
        lax.psum_scatter(grad_up_rows, "lon", scatter_dimension=0, tiled=True),
        lax.psum_scatter(grad_down, "lon", scatter_dimension=0, tiled=True),
    )
    up_part, down_part = lax.psum((up_part, down_part), "var")
    return (jnp.transpose(up_part), down_part)


def on_device(
    pixels, w_embed, level_embed, latents, w_query, w_key, w_value, w_out, w_up, w_down, cotangent
):
    lev_dev = pixels.shape[0]
    first_level = lax.axis_index("var") * lev_dev
    level_rows = lax.dynamic_slice_in_dim(level_embed, first_level, lev_dev, 0)
    own_tokens = embed_levels(pixels, w_embed, level_rows)
    tokens = lax.all_to_all(own_tokens, "var", split_axis=1, concat_axis=0, tiled=True)
    pooled, mlp_grads, saved = front(
        tokens, latents, w_query, w_key, w_value, w_out, w_up, w_down, cotangent
    )
    grad_out, grad_up_rows, grad_down = mlp_grads
    d_tokens, attn_grads = back(saved, latents, w_query, w_key, w_value, w_out)
    d_own = lax.all_to_all(d_tokens, "var", split_axis=0, concat_axis=1, tiled=True)
    grad_embed, level_part = embed_grads(pixels, d_own)
    grad_level = lax.dynamic_update_slice(
        jnp.zeros(level_embed.shape, F32), level_part, (first_level, 0)
    )
    grad_query, grad_key, grad_value, grad_lat = attn_grads
    summed = lax.psum(
        (grad_embed, grad_level, grad_lat, grad_query, grad_key, grad_value, grad_out),
        ("var", "lon"),
    )
    grad_embed, grad_level, grad_lat, grad_query, grad_key, grad_value, grad_out = summed
    grad_up, grad_down = ffn_sums(grad_up_rows, grad_down)
    return (
        pooled,
        grad_embed,
        grad_level,
        grad_lat,
        grad_query,
        grad_key,
        grad_value,
        grad_out,
        grad_up,
        grad_down,
    )


def solution(mesh):
    return jax.shard_map(
        on_device,
        mesh=mesh,
        in_specs=(
            P("var", None, None, "lon"),
            P(),
            P(),
            P(),
            P(),
            P(),
            P(),
            P(),
            P(),
            P(),
            P(None, ("lon", "var"), None),
        ),
        out_specs=(
            P(None, ("lon", "var"), None),
            P(),
            P(),
            P(),
            P(),
            P(),
            P(),
            P(),
            P(None, "lon"),
            P("lon", None),
        ),
        check_vma=False,
    )
```

profile of v0, /device:TPU:0, one launch (start us, length us, event | category | flops | bytes accessed | tf_op | source)
XLA Modules:
  0.0 465.6 jit_solution(16768565339959139172)
XLA Ops:
  13.8 8.0 %reduce.3 = bf16[1024,512]{1,0:T(8,128)(2,1)S(1)} reduce(bf16[1024,1,512]{2,1,0:T(2,128)(2,1)} %bitcast.154, bf16[]{:T(256)} %broadcast.130), dimensions={1}, to_apply=%bitcast.143.reduce_sub_computation | reduce | bytes 2097154
  23.4 5.9 %all-to-all-start = ((bf16[8,2,32768]{2,1,0:T(2,128)(2,1)}), bf16[8,2,32768]{2,1,0:T(2,128)(2,1)S(1)}, u32[]{:S(2)}, u32[]{:S(2)}) async-start(bf16[8,2,32768]{2,1,0:T(2,128)(2,1)} %reshape.215), calls=%async_computation | async-start | bytes 2097152 | tf_op jit(solution)/shard_map/all_to_all | solution.py:165
  31.7 13.3 %all-to-all-done = bf16[8,2,32768]{2,1,0:T(2,128)(2,1)S(1)} async-done(((bf16[8,2,32768]{2,1,0:T(2,128)(2,1)}), bf16[8,2,32768]{2,1,0:T(2,128)(2,1)S(1)}, u32[]{:S(2)}, u32[]{:S(2)}) %all-to-all-start) | async-done | bytes 1048608 | tf_op jit(solution)/shard_map/all_to_all | solution.py:165
  54.2 3.9 copy.96
  63.8 3.9 convolution_convert_fusion.1
  67.6 3.9 copy.95
  71.5 7.5 %copy.99 = bf16[8,128,16,64]{3,0,2,1:T(8,128)(2,1)} copy(bf16[8,128,16,64]{1,3,2,0:T(8,128)(2,1)} %bitcast.144) | data formatting | bytes 4194304 | tf_op jit(solution)/shard_map/reshape | solution.py:65
  79.0 6.5 %convert_bitcast_fusion.2 = bf16[3,128,16,64]{3,0,2,1:T(4,128)(2,1)} fusion(bf16[8,128,16,64]{3,0,2,1:T(8,128)(2,1)} %copy.99, bf16[16,3,8,128]{2,1,0,3:T(4,128)(2,1)} %copy.100), kind=kOutput, calls=%fused_computation.33 | convolution fusion | flops 6684672 | bytes 2981888 | tf_op jit(solution)/shard_map/hqlp,lphj->qphj/dot_general | solution.py:17
  85.5 4.2 copy.101
  98.3 5.2 %fusion.6 = bf16[3,128,2048]{2,1,0:T(8,128)(2,1)S(1)} fusion(f32[3,128,2048]{2,1,0:T(8,128)} %copy-done.12, bf16[3,128,512]{2,1,0:T(8,128)(2,1)} %param.21, bf16[2048,512]{1,0:T(8,128)(2,1)} %param.20), kind=kOutput, calls=%fused_computation.11 | convolution fusion | flops 821035008 | bytes 7208960 | tf_op jit(solution)/shard_map/dot_general | solution.py:29
  108.0 5.2 %copy.104 = bf16[8,128,16,64]{3,0,1,2:T(8,128)(2,1)} copy(bf16[8,128,16,64]{1,3,2,0:T(8,128)(2,1)} %bitcast.145) | data formatting | bytes 4194304 | tf_op jit(solution)/shard_map/reshape | solution.py:65
  113.2 4.5 copy.118
  129.3 6.4 %fusion.70 = f32[16,128,8,3]{2,3,1,0:T(4,128)} fusion(bf16[8,128,16,64]{3,0,1,2:T(8,128)(2,1)} %copy.104, bf16[3,128,16,64]{3,0,1,2:T(4,128)(2,1)S(1)} %copy.105), kind=kOutput, calls=%fused_computation.92 | convolution fusion | flops 6291456 | bytes 3080192 | tf_op jit(solution)/shard_map/qphj,lphj->hqlp/dot_general | solution.py:17
  135.7 4.5 copy.106
  150.0 4.2 convert_bitcast_fusion
  154.1 5.7 %copy.112 = bf16[8,128,16,64]{1,3,2,0:T(8,128)(2,1)S(1)} copy(bf16[8,128,16,64]{3,0,2,1:T(8,128)(2,1)} %convert_bitcast_fusion) | data formatting | bytes 4194304 | tf_op jit(solution)/shard_map/convert_element_type | solution.py:118
  166.8 3.6 all-to-all-start.1
  179.5 7.7 %copy.117 = bf16[8,128,16,64]{1,0,3,2:T(8,128)(2,1)} copy(bf16[8,128,16,64]{3,0,2,1:T(8,128)(2,1)} %convert_bitcast_fusion) | data formatting | bytes 4194304 | tf_op jit(solution)/shard_map/convert_element_type | solution.py:118
  187.2 4.8 %fusion.10 = f32[512,1024]{1,0:T(8,128)} fusion(bf16[128,8,8,128]{3,2,1,0:T(8,128)(2,1)} %bitcast.162, bf16[1,1024,512]{2,1,0:T(8,128)(2,1)S(1)} %copy-done.7, f32[1024]{0:T(1024)S(1)} %copy-done.31, f32[1024]{0:T(1024)S(1)} %copy-done.27), kind=kOutput, calls=%fused_computation.16 | convolution fusion | flops 1075838976 | bytes 5251072 | tf_op jit(solution)/shard_map/dot_general | solution.py:23
  196.3 65.8 %reduce-scatter.3.cloned.1.call-done = f32[128,512]{1,0:T(8,128)} async-done(((f32[2048,512]{1,0:T(8,128)}), f32[128,512]{1,0:T(8,128)}) %reduce-scatter.3.cloned.1.call-update) | async-done | bytes 262160 | tf_op jit(solution)/shard_map/reduce_scatter | solution.py:151
  262.2 4.5 fusion.30
  267.9 65.3 %all-reduce = (f32[8,512]{1,0:T(8,128)}, f32[3,512]{1,0:T(4,128)}) all-reduce(f32[8,512]{1,0:T(8,128)S(1)} %dynamic_update_slice.3, f32[3,512]{1,0:T(4,128)S(1)} %convolution_add_fusion.2), channel_id=1, replica_groups=mesh['var'=8,'lon'=16] {'var','lon'}, use_global_device_ids=true, to_apply=%region_9.0 | all-reduce | flops 5632 | bytes 45056 | tf_op jit(solution)/shard_map/psum | solution.py:177
  333.2 39.6 %all-reduce.6.cloned.1.call-done = (f32[80,512]{1,0:T(8,128)}, f32[512,1024]{0,1:T(8,128)}, f32[512,1024]{1,0:T(8,128)}, f32[512,1024]{1,0:T(8,128)}, f32[1024,512]{1,0:T(8,128)}) async-done(((f32[80,512]{1,0:T(8,128)}, f32[512,1024]{0,1:T(8,128)}, f32[512,1024]{1,0:T(8,128)}, f32[512,1024]{1,0:T(8,128)}, f32[1024,512]{1,0:T(8,128)}), (f32[80,512]{1,0:T(8,128)}, f32[512,1024]{0,1:T(8,128)}, ...) | async-done | bytes 8552464 | tf_op jit(solution)/shard_map/psum | solution.py:177
  375.8 73.0 %all-reduce.8.cloned.1.call-done = (f32[512,128]{0,1:T(8,128)}, f32[128,512]{1,0:T(8,128)}) async-done(((f32[512,128]{0,1:T(8,128)}, f32[128,512]{1,0:T(8,128)}), (f32[512,128]{0,1:T(8,128)}, f32[128,512]{1,0:T(8,128)})) %all-reduce.8.cloned.1.call-update) | async-done | bytes 524304 | tf_op jit(solution)/shard_map/psum | solution.py:154
  (134 shorter events, 92.6 us)
Async XLA Ops:
  8.0 83.7 %copy-start = (bf16[512,2048]{1,0:T(8,128)(2,1)S(1)}, bf16[512,2048]{1,0:T(8,128)(2,1)}, u32[]{:S(2)}) copy-start(bf16[512,2048]{1,0:T(8,128)(2,1)} %param.19) | copy-start | bytes 6291460
  21.8 7.7 %copy-start.24 = (bf16[3,512]{1,0:T(4,128)(2,1)S(1)}, bf16[3,512]{1,0:T(4,128)(2,1)}, u32[]{:S(2)}) copy-start(bf16[3,512]{1,0:T(4,128)(2,1)} %param.14) | copy-start | bytes 9220
  23.4 21.6 %all-to-all-start = ((bf16[8,2,32768]{2,1,0:T(2,128)(2,1)}), bf16[8,2,32768]{2,1,0:T(2,128)(2,1)S(1)}, u32[]{:S(2)}, u32[]{:S(2)}) async-start(bf16[8,2,32768]{2,1,0:T(2,128)(2,1)} %reshape.215), calls=%async_computation | async-start | bytes 2097152 | tf_op jit(solution)/shard_map/all_to_all | solution.py:165
  29.3 167.0 %reduce-scatter.5.cloned.1.call-start = ((), (), s32[]{:S(2)}) async-start(), calls=%async_computation.5 | async-start | bytes 4456448 | tf_op jit(solution)/shard_map/reduce_scatter | solution.py:152
  50.3 114.9 %copy-start.6 = (bf16[1,1024,512]{2,1,0:T(8,128)(2,1)}, bf16[1,1024,512]{2,1,0:T(8,128)(2,1)S(1)}, u32[]{:S(2)}) copy-start(bf16[1,1024,512]{2,1,0:T(8,128)(2,1)S(1)} %get-tuple-element.64) | copy-start | bytes 3145732
  50.4 3.8 copy-start.26
  51.5 12.3 %copy-start.28 = (f32[8,128]{1,0:T(8,128)}, f32[8,128]{1,0:T(8,128)S(1)}, u32[]{:S(2)}) copy-start(f32[8,128]{1,0:T(8,128)S(1)} %get-tuple-element.68) | copy-start | bytes 12292
  97.9 164.2 %reduce-scatter.3.cloned.1.call-start = ((), (), s32[]{:S(2)}) async-start(), calls=%async_computation.4 | async-start | bytes 4456448 | tf_op jit(solution)/shard_map/reduce_scatter | solution.py:151
  117.7 4.0 copy-start.17
  135.7 6.8 %copy-start.8 = (bf16[8,128,1024]{1,2,0:T(8,128)(2,1)S(1)}, bf16[8,128,1024]{1,2,0:T(8,128)(2,1)}, u32[]{:S(2)}) copy-start(bf16[8,128,1024]{1,2,0:T(8,128)(2,1)} %copy.96) | copy-start | bytes 6291460
  166.8 28.1 %all-to-all-start.1 = ((bf16[8,128,512]{2,1,0:T(8,128)(2,1)}), bf16[8,128,512]{2,1,0:T(8,128)(2,1)S(1)}, u32[]{:S(2)}, u32[]{:S(2)}) async-start(bf16[8,128,512]{2,1,0:T(8,128)(2,1)} %multiply_convert_fusion.2), calls=%async_computation.1 | async-start | bytes 2097152 | tf_op jit(solution)/shard_map/all_to_all | solution.py:171
  170.4 3.6 copy-start.23
  170.4 202.4 %all-reduce.6.cloned.1.call-start = ((), (), s32[]{:S(2)}) async-start(), calls=%async_computation.6 | async-start | bytes 17104896 | tf_op jit(solution)/shard_map/psum | solution.py:177
  170.5 5.9 %copy-start.4 = (bf16[8,128,16,64]{1,3,0,2:T(8,128)(2,1)S(1)}, bf16[8,128,16,64]{1,3,0,2:T(8,128)(2,1)}, u32[]{:S(2)}) copy-start(bf16[8,128,16,64]{1,3,0,2:T(8,128)(2,1)} %copy-done.3) | copy-start | bytes 6291460
  179.5 7.7 %copy-start.7 = (bf16[1,1024,512]{2,1,0:T(8,128)(2,1)S(1)}, bf16[1,1024,512]{2,1,0:T(8,128)(2,1)}, u32[]{:S(2)}) copy-start(bf16[1,1024,512]{2,1,0:T(8,128)(2,1)} %copy-done.6) | copy-start | bytes 3145732
  179.5 7.7 %copy-start.27 = (f32[1024]{0:T(1024)S(1)}, f32[1024]{0:T(1024)}, u32[]{:S(2)}) copy-start(f32[1024]{0:T(1024)} %copy-done.26) | copy-start | bytes 12292
  179.5 7.7 %copy-start.31 = (f32[1024]{0:T(1024)S(1)}, f32[1024]{0:T(1024)}, u32[]{:S(2)}) copy-start(f32[1024]{0:T(1024)} %get-tuple-element.67) | copy-start | bytes 12292
  187.2 4.8 %copy-start.13 = (bf16[8,128,16,64]{1,0,3,2:T(8,128)(2,1)S(1)}, bf16[8,128,16,64]{1,0,3,2:T(8,128)(2,1)}, u32[]{:S(2)}) copy-start(bf16[8,128,16,64]{1,0,3,2:T(8,128)(2,1)} %copy.117) | copy-start | bytes 6291460
  196.0 252.8 %all-reduce.8.cloned.1.call-start = ((), (), s32[]{:S(2)}) async-start(), calls=%async_computation.7 | async-start | bytes 1048576 | tf_op jit(solution)/shard_map/psum | solution.py:154
  262.1 4.6 copy-start.10
  262.1 4.5 copy-start.30
  372.8 77.8 %copy-start.22 = (f32[80,512]{1,0:T(8,128)S(1)}, f32[80,512]{1,0:T(8,128)}, u32[]{:S(2)}) copy-start(f32[80,512]{1,0:T(8,128)} %get-tuple-element.78) | copy-start | bytes 491524
  372.8 78.5 %copy-start.16 = (f32[512,1024]{1,0:T(8,128)S(1)}, f32[512,1024]{1,0:T(8,128)}, u32[]{:S(2)}) copy-start(f32[512,1024]{1,0:T(8,128)} %get-tuple-element.82) | copy-start | bytes 6291460
  453.6 4.4 copy-start.1
  (17 other events, 36.7 us)
Sparse Core Ops, SparseCore 0:
  98.0 80.0 reduce-scatter.4
  182.1 79.9 reduce-scatter.2
Sparse Core Ops, SparseCore 1:
  196.1 176.7 all-reduce.5
  375.3 73.4 all-reduce.7
where the time goes:
time: 473 us; the launch traced here: 466 us
  waiting for transfers between devices  192 us (41%)
  local copies, waits for them, and re-layouts  89.5 us (19%)
  matrix products  75 us (16%)
  blocking collectives  65.3 us (14%)
  other arithmetic  17.5 us (4%)
  between operations  16.1 us (3%)
  starting transfers between devices  10.4 us (2%)
    psum x1, waiting for transfers between devices, ffn_sums(): up_part, down_part = lax.psum((up_part, down_part), 'var')  73 us
    reduce_scatter x1, waiting for transfers between devices, ffn_sums(): lax.psum_scatter(grad_up_rows, 'lon', scatter_dimension=0, tiled=True)  65.8 us
    psum x1, blocking collectives, on_device(): lax.psum((grad_embed, grad_level, grad_lat, grad_query, grad_key, grad_va...  65.3 us
    psum x1, waiting for transfers between devices, on_device(): lax.psum((grad_embed, grad_level, grad_lat, grad_query, grad_key, grad_va...  39.6 us
    unnamed x80, local copies, waits for them, and re-layouts  25.2 us
    dot_general x6, matrix products, contract(): return jnp.einsum(form, left, right, preferred_element_type=F32)  21.4 us
    dot_general x5, matrix products, flat_outer(): lax.dot_general(left_rows, right_rows, (((0,), (0,)), ((), ())), preferre...  18 us
    dot_general x5, matrix products, times_transposed(): lax.dot_general(left, weight, (((left.ndim - 1,), (1,)), ((), ())), prefe...  14.4 us
  transfers between devices with their start and end apart: 6, of which 4 were waited for; matrix products, arithmetic and copies ran while one was open for 21% of the time, Pallas kernels for 0%

commit v1 on v0

v1 whole, which is shorter than its diff:
```python
import functools
import math

import jax
import jax.numpy as jnp
from jax import lax
from jax.experimental import pallas as pl
from jax.experimental.pallas import tpu as pltpu
from jax.sharding import PartitionSpec as P

F32 = jnp.float32
BF16 = jnp.bfloat16
EPSILON = 1e-05
HEADS = 16
HEAD = 64
LEV = 8
LAT = 3
ROWS = 128
TILE = 256
PAD = 128
SMALL = 192
GELU_C = math.sqrt(2.0 / math.pi)
GELU_A = 0.044715


def mm(left, right):
    return lax.dot_general(left, right, (((1,), (0,)), ((), ())), preferred_element_type=F32)


def mm_nt(left, right):
    return lax.dot_general(left, right, (((1,), (1,)), ((), ())), preferred_element_type=F32)


def mm_tn(left, right):
    return lax.dot_general(left, right, (((0,), (0,)), ((), ())), preferred_element_type=F32)


def split(value):
    high = value.astype(BF16)
    return high, (value - high.astype(F32)).astype(BF16)


def head_rows(inner):
    row = lax.broadcasted_iota(jnp.int32, (PAD, inner), 0)
    head = lax.broadcasted_iota(jnp.int32, (PAD, inner), 1) // HEAD
    return row, head


def query_rows(latents, w_query):
    queries = mm(latents, w_query).astype(BF16).astype(F32)
    inner = queries.shape[1]
    row, head = head_rows(inner)
    spread = jnp.zeros((PAD, inner), F32)
    for q in range(LAT):
        spread = jnp.where(row == q * HEADS + head, queries[q : q + 1, :], spread)
    return spread.astype(BF16)


def prepare(latents, w_query, w_key, select, wq_high, wq_low):
    inner = w_key.shape[1]
    row, head = head_rows(inner)
    for q in range(LAT):
        select[q] = jnp.where(row == q * HEADS + head, 1.0, 0.0).astype(BF16)
    folded = mm_nt(query_rows(latents[...], w_query[...]), w_key[...])
    high, low = split(folded)
    wq_high[...] = high
    wq_low[...] = low


def forward(
    px, w_embed, level_embed, w_value, wq_high, wq_low, level_rows, unit, inv, normed, normed_t, values, scores
):
    level_rows[...] = level_embed[...].astype(F32)

    @pl.loop(0, LEV)
    def _(l):
        token = mm_tn(px[l], w_embed[...]) + level_rows[pl.ds(l, 1), :]
        token = token.astype(BF16).astype(F32)
        center = token - jnp.mean(token, axis=-1, keepdims=True)
        inverse = lax.rsqrt(jnp.mean(center * center, axis=-1, keepdims=True) + EPSILON)
        own = center * inverse
        unit[l] = own
        inv[l] = jnp.broadcast_to(inverse, (ROWS, PAD))
        own = own.astype(BF16)
        normed[pl.ds(pl.multiple_of(l * ROWS, ROWS), ROWS), :] = own
        scores[l] = (mm_nt(own, wq_high[...]) + mm_nt(own, wq_low[...])) * (1.0 / math.sqrt(HEAD))
        values[l] = mm(own, w_value[...]).astype(BF16)

    normed_t[...] = normed[...].T


def softmax(scores, weights):
    highest = scores[0]
    for l in range(1, LEV):
        highest = jnp.maximum(highest, scores[l])
    total = jnp.zeros_like(highest)
    for l in range(LEV):
        expo = jnp.exp(scores[l] - highest)
        scores[l] = expo
        total = total + expo
    for l in range(LEV):
        prob = scores[l] / total
        scores[l] = prob
        weights[l * ROWS : (l + 1) * ROWS, :] = prob.astype(BF16)


def mix(weights, select, values, spread, mixed):
    inner = values.shape[2]

    @pl.loop(0, inner // TILE)
    def _(t):
        cols = pl.ds(pl.multiple_of(t * TILE, TILE), TILE)
        for q in range(LAT):
            total = jnp.zeros((ROWS, TILE), F32)
            for l in range(LEV):
                own = mm(weights[l * ROWS : (l + 1) * ROWS, :], select[q, :, cols])
                spread[q, l, :, cols] = own.astype(BF16)
                total = total + own * values[l, :, cols].astype(F32)
            mixed[q * ROWS : (q + 1) * ROWS, cols] = total.astype(BF16)


def attend(latents, mixed, w_out, attended):
    for q in range(LAT):
        rows = slice(q * ROWS, (q + 1) * ROWS)
        own = mm(mixed[rows, :], w_out[...]) + latents[q : q + 1, :].astype(F32)
        attended[rows, :] = own.astype(BF16)


def feed_forward(attended, cot, w_up, w_down, pool_sum, d_att, put_up, put_down):
    pool_sum[...] = attended[...].astype(F32)
    d_att[...] = cot[...].astype(F32)

    @pl.loop(0, w_up.shape[1] // TILE)
    def _(t):
        cols = pl.ds(pl.multiple_of(t * TILE, TILE), TILE)
        pre = mm(attended[...], w_up[:, cols])
        square = pre * pre
        bent = jnp.tanh(GELU_C * (pre + GELU_A * (square * pre)))
        half = 0.5 * (1.0 + bent)
        hidden = (pre * half).astype(BF16)
        slope = half + 0.5 * pre * (1.0 - bent * bent) * (GELU_C * (1.0 + 3.0 * GELU_A * square))
        d_pre = (mm_nt(cot[...], w_down[cols, :]) * slope).astype(BF16)
        pool_sum[...] += mm(hidden, w_down[cols, :])
        d_att[...] += mm_nt(d_pre, w_up[:, cols])
        put_down(t, mm_tn(hidden, cot[...]).astype(BF16))
        put_up(t, mm_tn(d_pre, attended[...]).astype(BF16))


def value_back(spread, d_mixed, values, normed_t, select, d_values, d_weights, put_value):
    inner = values.shape[2]
    d_weights[...] = jnp.zeros_like(d_weights)

    @pl.loop(0, inner // TILE)
    def _(t):
        cols = pl.ds(pl.multiple_of(t * TILE, TILE), TILE)
        for l in range(LEV):
            rows = slice(l * ROWS, (l + 1) * ROWS)
            own = values[l, :, cols].astype(F32)
            total = jnp.zeros((ROWS, TILE), F32)
            back = jnp.zeros((ROWS, PAD), F32)
            for q in range(LAT):
                d_mix = d_mixed[q * ROWS : (q + 1) * ROWS, cols].astype(F32)
                total = total + spread[q, l, :, cols].astype(F32) * d_mix
                back = back + mm_nt((d_mix * own).astype(BF16), select[q, :, cols])
            d_values[rows, cols] = total.astype(BF16)
            d_weights[rows, :] += back
        put_value(t, mm(normed_t[...], d_values[:, cols]).astype(BF16))


def score_back(probs, d_weights, d_scores):
    total = jnp.zeros((ROWS, PAD), F32)
    for l in range(LEV):
        total = total + probs[l] * d_weights[l * ROWS : (l + 1) * ROWS, :]
    for l in range(LEV):
        rows = slice(l * ROWS, (l + 1) * ROWS)
        own = probs[l] * (d_weights[rows, :] - total) * (1.0 / math.sqrt(HEAD))
        d_scores[rows, :] = own.astype(BF16)


def token_back(px, unit, inv, w_value, wq_high, d_values, d_scores, small):
    small[48:SMALL, :] = jnp.zeros((SMALL - 48, small.shape[1]), F32)

    @pl.loop(0, LEV)
    def _(l):
        rows = pl.ds(pl.multiple_of(l * ROWS, ROWS), ROWS)
        d_normed = mm_nt(d_values[rows, :], w_value[...]) + mm(d_scores[rows, :], wq_high[...])
        own = unit[l]
        inverse = inv[l][:, :1]
        d_token = inverse * (
            d_normed
            - jnp.mean(d_normed, axis=-1, keepdims=True)
            - own * jnp.mean(d_normed * own, axis=-1, keepdims=True)
        )
        d_token = d_token.astype(BF16)
        small[48:128, :] += mm(px[l], d_token)
        small[pl.ds(128 + l, 1), :] = jnp.sum(d_token.astype(F32), axis=0, keepdims=True)


def local_kernel(
    px, w_embed, level_embed, latents, w_query, w_key, w_value, w_out, w_up, w_down, cot,
    pooled, up_all, down_all, out_all, value_all, small,
    select, wq_high, wq_low, level_rows, unit, inv, normed, normed_t, values, scores, weights, spread, mixed,
    attended, pool_sum, d_att, d_att_b, d_mixed, d_values, d_weights, d_scores,
):
    prepare(latents, w_query, w_key, select, wq_high, wq_low)
    forward(
        px, w_embed, level_embed, w_value, wq_high, wq_low, level_rows, unit, inv, normed, normed_t, values, scores
    )
    softmax(scores, weights)
    mix(weights, select, values, spread, mixed)
    attend(latents, mixed, w_out, attended)

    def put_up(t, block):
        up_all[pl.ds(pl.multiple_of(t * TILE, TILE), TILE), :] = block

    def put_down(t, block):
        down_all[pl.ds(pl.multiple_of(t * TILE, TILE), TILE), :] = block

    def put_value(t, block):
        value_all[t] = block

    feed_forward(attended, cot, w_up, w_down, pool_sum, d_att, put_up, put_down)
    pooled[...] = pool_sum[...].astype(BF16)
    d_att_b[...] = d_att[...].astype(BF16)
    d_mixed[...] = mm_nt(d_att_b[...], w_out[...]).astype(BF16)
    for half in range(2):
        out_all[half] = mm_tn(mixed[...], d_att_b[:, half * TILE : (half + 1) * TILE]).astype(BF16)
    value_back(spread, d_mixed, values, normed_t, select, d_values, d_weights, put_value)
    score_back(scores, d_weights, d_scores)
    token_back(px, unit, inv, w_value, wq_high, d_values, d_scores, small)
    small[0:48, :] = mm_tn(d_scores[...], normed[...])[0:48, :]
    for q in range(LAT):
        small[136 + q : 137 + q, :] = jnp.sum(d_att[q * ROWS : (q + 1) * ROWS, :], axis=0, keepdims=True)


def local_part(px, w_embed, level_embed, latents, w_query, w_key, w_value, w_out, w_up, w_down, cot):
    width, inner, ffn = w_key.shape[0], w_key.shape[1], w_up.shape[1]
    every, pairs = LEV * ROWS, LAT * ROWS
    shape = jax.ShapeDtypeStruct
    whole = pl.BlockSpec(memory_space=pltpu.VMEM)
    return pl.pallas_call(
        local_kernel,
        out_shape=(
            shape((pairs, width), BF16),
            shape((ffn, width), BF16),
            shape((ffn, width), BF16),
            shape((2, inner, TILE), BF16),
            shape((4, width, TILE), BF16),
            shape((SMALL, width), F32),
        ),
        in_specs=[whole] * 11,
        out_specs=(whole,) * 6,
        scratch_shapes=[
            pltpu.VMEM((LAT, PAD, inner), BF16),
            pltpu.VMEM((PAD, width), BF16),
            pltpu.VMEM((PAD, width), BF16),
            pltpu.VMEM((LEV, width), F32),
            pltpu.VMEM((LEV, ROWS, width), F32),
            pltpu.VMEM((LEV, ROWS, PAD), F32),
            pltpu.VMEM((every, width), BF16),
            pltpu.VMEM((width, every), BF16),
            pltpu.VMEM((LEV, ROWS, inner), BF16),
            pltpu.VMEM((LEV, ROWS, PAD), F32),
            pltpu.VMEM((every, PAD), BF16),
            pltpu.VMEM((LAT, LEV, ROWS, inner), BF16),
            pltpu.VMEM((pairs, inner), BF16),
            pltpu.VMEM((pairs, width), BF16),
            pltpu.VMEM((pairs, width), F32),
            pltpu.VMEM((pairs, width), F32),
            pltpu.VMEM((pairs, width), BF16),
            pltpu.VMEM((pairs, inner), BF16),
            pltpu.VMEM((every, inner), BF16),
            pltpu.VMEM((every, PAD), F32),
            pltpu.VMEM((every, PAD), BF16),
        ],
        compiler_params=pltpu.CompilerParams(vmem_limit_bytes=60 * 1024 * 1024),
        name="local_part",
    )(px, w_embed, level_embed, latents, w_query, w_key, w_value, w_out, w_up, w_down, cot)


def finish_kernel(
    small, value_all, out_all, latents, w_query, w_key,
    grad_embed, grad_level, grad_lat, grad_query, grad_key, grad_value, grad_out,
):
    grad_embed[...] = small[48:128, :].astype(F32)
    grad_level[...] = small[128:136, :].astype(F32)
    for t in range(4):
        grad_value[:, t * TILE : (t + 1) * TILE] = value_all[t].astype(F32)
    for half in range(2):
        grad_out[:, half * TILE : (half + 1) * TILE] = out_all[half].astype(F32)
    rows = query_rows(latents[...], w_query[...])
    high, low = split(small[0:48, :].astype(F32))
    grad_key[...] = mm_tn(high, rows[0:48, :]) + mm_tn(low, rows[0:48, :])
    spread = mm(high, w_key[...]) + mm(low, w_key[...])
    inner = w_key.shape[1]
    row = lax.broadcasted_iota(jnp.int32, (48, inner), 0)
    head = lax.broadcasted_iota(jnp.int32, (48, inner), 1) // HEAD
    own = []
    for q in range(LAT):
        own.append(jnp.sum(jnp.where(row == q * HEADS + head, spread, 0.0), axis=0, keepdims=True))
    d_queries = jnp.concatenate(own, axis=0)
    high, low = split(d_queries)
    grad_query[...] = mm_tn(latents[...], high) + mm_tn(latents[...], low)
    grad_lat[...] = small[136:139, :].astype(F32) + mm_nt(high, w_query[...]) + mm_nt(low, w_query[...])


def finish(small, value_all, out_all, latents, w_query, w_key):
    width, inner = w_key.shape
    shape = jax.ShapeDtypeStruct
    whole = pl.BlockSpec(memory_space=pltpu.VMEM)
    return pl.pallas_call(
        finish_kernel,
        out_shape=(
            shape((80, width), F32),
            shape((LEV, width), F32),
            shape((LAT, width), F32),
            shape((width, inner), F32),
            shape((width, inner), F32),
            shape((width, inner), F32),
            shape((inner, width), F32),
        ),
        in_specs=[whole] * 6,
        out_specs=(whole,) * 7,
        compiler_params=pltpu.CompilerParams(vmem_limit_bytes=60 * 1024 * 1024),
        name="finish",
    )(small, value_all, out_all, latents, w_query, w_key)


def on_device(
    pixels, w_embed, level_embed, latents, w_query, w_key, w_value, w_out, w_up, w_down, cotangent
):
    width = w_embed.shape[1]
    own = pixels.reshape(80, LEV, ROWS)
    px = lax.all_to_all(own, "var", split_axis=1, concat_axis=1, tiled=True)
    px = jnp.transpose(px, (1, 0, 2))
    pooled, up_all, down_all, out_all, value_all, small = local_part(
        px, w_embed, level_embed, latents, w_query, w_key, w_value, w_out, w_up, w_down,
        cotangent.reshape(LAT * ROWS, width),
    )
    both = jnp.concatenate(
        [up_all.reshape(16, -1, width), down_all.reshape(16, -1, width)], axis=1
    )
    part = lax.psum_scatter(both, "lon", scatter_dimension=0, tiled=True)
    part = lax.psum(part, "var")[0].astype(F32)
    up_part, down_part = part[:ROWS], part[ROWS:]
    small, value_all, out_all = lax.psum((small.astype(BF16), value_all, out_all), ("var", "lon"))
    grads = finish(small, value_all, out_all, latents, w_query, w_key)
    return (pooled.reshape(LAT, ROWS, width), *grads, jnp.transpose(up_part), down_part)


def solution(mesh):
    return jax.shard_map(
        on_device,
        mesh=mesh,
        in_specs=(
            P("var", None, None, "lon"),
            *([P()] * 9),
            P(None, ("lon", "var"), None),
        ),
        out_specs=(
            P(None, ("lon", "var"), None),
            *([P()] * 7),
            P(None, "lon"),
            P("lon", None),
        ),
        check_vma=False,
    )
```

time: 473 us -> 318 us (0.67); the launches traced: 466 us -> 317 us
  local copies, waits for them, and re-layouts: 89.5 us -> 3.46 us
  matrix products: 75 us -> 0 us
  blocking collectives: 65.3 us -> 12.6 us
  Pallas kernels: 0 us -> 44.3 us
  waiting for transfers between devices: 192 us -> 235 us
  other arithmetic: 17.5 us -> 6.24 us
  starting transfers between devices: 10.4 us -> 0.13 us
    dot_general x26 -> x0, matrix products: 75 us -> none  [the longest x6 21.4 us: contract(): return jnp.einsum(form, left, right, preferred_element_type=F32)]
    psum x1 -> x0, blocking collectives: 65.3 us -> none  [on_device(): lax.psum((grad_embed, grad_level, grad_lat, grad_query, grad_key, grad_va...]
    pallas_call x0 -> x2, Pallas kernels: none -> 44.3 us  [the longest x1 36.5 us: local_part(): pl.pallas_call(local_kernel, out_shape=(shape((pairs, width), BF16), shap...]
    psum x2, waiting for transfers between devices: 113 us -> 156 us  [the longest x1 89.1 us: on_device(): lax.psum((small.astype(BF16), value_all, out_all), ('var', 'lon'))]
    convert_element_type x11 -> x0, local copies, waits for them, and re-layouts: 40.6 us -> none  [the longest x2 13.4 us: back(): contract('hqlp,qphj->lphj', weights, d_mixed).astype(BF16)]
    unnamed x80 -> x4, local copies, waits for them, and re-layouts: 25.2 us -> 2.7 us
    reshape x6 -> x1, local copies, waits for them, and re-layouts: 19.1 us -> 0.02 us  [on_device(): own = pixels.reshape(80, LEV, ROWS)]
    all_to_all x2 -> x0, waiting for transfers between devices: 13.3 us -> none  [the longest x1 13.3 us: on_device(): lax.all_to_all(own_tokens, 'var', split_axis=1, concat_axis=0, tiled=True)]
  transfers between devices with their start and end apart: 6 -> 3, of which waited for: 4 -> 3; matrix products, arithmetic and copies ran while one was open for 21% -> 0% of each run, Pallas kernels for 0% -> 2%
where the time goes in v1:
time: 318 us; the launch traced here: 317 us
  waiting for transfers between devices  235 us (74%)
  Pallas kernels  44.3 us (14%)
  between operations  15.5 us (5%)
  blocking collectives  12.6 us (4%)
  other arithmetic  6.24 us (2%)
  local copies, waits for them, and re-layouts  3.46 us (1%)
    psum x1, waiting for transfers between devices, on_device(): lax.psum((small.astype(BF16), value_all, out_all), ('var', 'lon'))  89.1 us
    reduce_scatter x1, waiting for transfers between devices, on_device(): part = lax.psum_scatter(both, 'lon', scatter_dimension=0, tiled=True)  79 us
    psum x1, waiting for transfers between devices, on_device(): part = lax.psum(part, 'var')[0].astype(F32)  66.9 us
    pallas_call x1, Pallas kernels, local_part(): pl.pallas_call(local_kernel, out_shape=(shape((pairs, width), BF16), shap...  36.5 us
    all_to_all x1, blocking collectives, on_device(): px = lax.all_to_all(own, 'var', split_axis=1, concat_axis=1, tiled=True)  12.6 us
    pallas_call x1, Pallas kernels, finish(): pl.pallas_call(finish_kernel, out_shape=(shape((80, width), F32), shape((...  7.79 us
  transfers between devices with their start and end apart: 3, of which 3 were waited for; matrix products, arithmetic and copies ran while one was open for 0% of the time, Pallas kernels for 2%

profile of v1, /device:TPU:0, one launch (start us, length us, event | category | flops | bytes accessed | tf_op | source)
XLA Modules:
  0.0 317.4 jit_solution(1472594747612734167)
XLA Ops:
  8.0 0.0 reduce-scatter.2.cloned.1.call-start
  8.1 0.9 copy.24
  9.0 12.6 %all_to_all.5 = bf16[80,8,128]{2,0,1:T(8,128)(2,1)} all-to-all(bf16[80,8,128]{2,0,1:T(8,128)(2,1)S(1)} %copy.22), channel_id=1, replica_groups=mesh['var'=8,'lon'=16] {'var'}, dimensions={1} | all-to-all | bytes 327680 | tf_op jit(solution)/shard_map/all_to_all | solution.py:334
  21.6 36.5 %local_part.1 = (bf16[384,512]{1,0:T(8,128)(2,1)}, bf16[2048,512]{1,0:T(8,128)(2,1)}, bf16[2048,512]{1,0:T(8,128)(2,1)}, bf16[2,1024,256]{2,1,0:T(8,128)(2,1)}, ...) custom-call(bf16[8,80,128]{2,1,0:T(8,128)(2,1)} %bitcast.18, bf16[80,512]{1,0:T(8,128)(2,1)} %w_embed.1, ...), custom_call_target="tpu_custom_call" | custom-call | tf_op jit(solution)/shard_map/local_part/pallas_call | solution.py:241
  58.1 4.5 %pad_maximum_fusion = bf16[16,256,512]{2,1,0:T(8,128)(2,1)} fusion(bf16[16,128,512]{2,1,0:T(8,128)(2,1)} %bitcast.16, bf16[16,128,512]{2,1,0:T(8,128)(2,1)} %bitcast.15), kind=kLoop, calls=%fused_computation | loop fusion | flops 8388608 | bytes 8388608 | tf_op jit(solution)/shard_map/concatenate | solution.py:340
  62.7 0.0 copy-start
  62.7 0.0 reduce-scatter.2.cloned.1.call-update
  62.7 0.0 all-reduce.6.cloned.1.call-start
  62.7 0.9 copy-done
  63.7 0.7 convert_element_type.7
  64.4 0.0 all-reduce.6.cloned.1.call-update
  64.4 0.0 all-reduce.4.cloned.1.call-start
  64.4 79.0 %reduce-scatter.2.cloned.1.call-done = bf16[1,256,512]{2,1,0:T(8,128)(2,1)} async-done(((bf16[16,256,512]{2,1,0:T(8,128)(2,1)}), bf16[1,256,512]{2,1,0:T(8,128)(2,1)}) %reduce-scatter.2.cloned.1.call-update) | async-done | bytes 262160 | tf_op jit(solution)/shard_map/reduce_scatter | solution.py:343
  143.5 0.0 all-reduce.4.cloned.1.call-update
  143.5 89.1 %all-reduce.6.cloned.1.call-done = (bf16[192,512]{1,0:T(8,128)(2,1)}, bf16[4,512,256]{2,1,0:T(8,128)(2,1)}, bf16[2,1024,256]{2,1,0:T(8,128)(2,1)}) async-done(((bf16[192,512]{1,0:T(8,128)(2,1)}, bf16[4,512,256]{2,1,0:T(8,128)(2,1)}, bf16[2,1024,256]{2,1,0:T(8,128)(2,1)}), (bf16[192,512]{1,0:T(8,128)(2,1)}, bf16[4,512,256]{2,1,0:T(8,128)(2,1)}, bf16[2,1024,256]{2,1,0:T(8,128)(2,1)})) %all-reduce.6.cloned.1.call-update) | async-done | bytes 2293776 | tf_op jit(solution)/shard_map/psum | solution.py:346
  232.7 7.8 %finish.1 = (f32[80,512]{1,0:T(8,128)}, f32[8,512]{1,0:T(8,128)}, f32[3,512]{1,0:T(4,128)}, f32[512,1024]{1,0:T(8,128)}, f32[512,1024]{1,0:T(8,128)}, /*index=5*/f32[512,1024]{1,0:T(8,128)}, f32[1024,512]{1,0:T(8,128)}) custom-call(bf16[192,512]{1,0:T(8,128)(2,1)} %get-tuple-element.56.small, bf16[4,512,256]{2,1,0:T(8,128)(2,1)} %get-tuple-element.57.value_all, ...), custom_call_target="tpu_custom_call" | custom-call | tf_op jit(solution)/shard_map/finish/pallas_call | solution.py:311
  240.5 66.9 %all-reduce.4.cloned.1.call-done = bf16[1,256,512]{2,1,0:T(8,128)(2,1)} async-done(((bf16[1,256,512]{2,1,0:T(8,128)(2,1)}), bf16[1,256,512]{2,1,0:T(8,128)(2,1)}) %all-reduce.4.cloned.1.call-update) | async-done | bytes 262160 | tf_op jit(solution)/shard_map/psum | solution.py:344
  307.4 1.0 convert_element_type.8
  308.4 0.7 slice_bitcast_fusion
  309.1 0.8 copy.23
  (1 shorter events, 0.0 us)
Async XLA Ops:
  8.0 135.5 %reduce-scatter.2.cloned.1.call-start = ((), (), s32[]{:S(2)}) async-start(), calls=%async_computation.2 | async-start | bytes 4456448 | tf_op jit(solution)/shard_map/reduce_scatter | solution.py:343
  62.7 1.0 copy-start
  62.7 170.0 %all-reduce.6.cloned.1.call-start = ((), (), s32[]{:S(2)}) async-start(), calls=%async_computation.4 | async-start | bytes 4587520 | tf_op jit(solution)/shard_map/psum | solution.py:346
  64.4 243.0 %all-reduce.4.cloned.1.call-start = ((), (), s32[]{:S(2)}) async-start(), calls=%async_computation.3 | async-start | bytes 524288 | tf_op jit(solution)/shard_map/psum | solution.py:344
Sparse Core Ops, SparseCore 0:
  62.8 80.6 reduce-scatter.1
Sparse Core Ops, SparseCore 1:
  69.6 163.0 all-reduce.5
  235.0 72.3 all-reduce.3

commit v2 on v1

--- a/solution.py
+++ b/solution.py
@@ -198,9 +198,9 @@
 
 def local_kernel(
     px, w_embed, level_embed, latents, w_query, w_key, w_value, w_out, w_up, w_down, cot,
-    pooled, up_all, down_all, out_all, value_all, small,
+    pooled, up_all, down_all, out_all, value_all, small_all,
     select, wq_high, wq_low, level_rows, unit, inv, normed, normed_t, values, scores, weights, spread, mixed,
-    attended, pool_sum, d_att, d_att_b, d_mixed, d_values, d_weights, d_scores,
+    attended, pool_sum, d_att, d_att_b, d_mixed, d_values, d_weights, d_scores, small,
 ):
     prepare(latents, w_query, w_key, select, wq_high, wq_low)
     forward(
@@ -211,26 +211,36 @@
     attend(latents, mixed, w_out, attended)
 
     def put_up(t, block):
-        up_all[pl.ds(pl.multiple_of(t * TILE, TILE), TILE), :] = block
+        for core in range(2):
+            for z_lo in range(2):
+                for y in range(4):
+                    start = core * 128 + z_lo * 64 + y * 16
+                    up_all[core, t // 2, y, t % 2 * 2 + z_lo] = block[start : start + 16]
 
     def put_down(t, block):
-        down_all[pl.ds(pl.multiple_of(t * TILE, TILE), TILE), :] = block
+        for core in range(2):
+            for z_lo in range(2):
+                for y in range(4):
+                    start = core * 128 + z_lo * 64 + y * 16
+                    down_all[core, y, t % 2 * 2 + z_lo, t // 2] = block[start : start + 16]
 
     def put_value(t, block):
-        value_all[t] = block
+        value_all[t // 2, pl.ds(t % 2 * 2, 2)] = block.reshape(2, 4, 4, 16, TILE)
 
     feed_forward(attended, cot, w_up, w_down, pool_sum, d_att, put_up, put_down)
     pooled[...] = pool_sum[...].astype(BF16)
     d_att_b[...] = d_att[...].astype(BF16)
     d_mixed[...] = mm_nt(d_att_b[...], w_out[...]).astype(BF16)
     for half in range(2):
-        out_all[half] = mm_tn(mixed[...], d_att_b[:, half * TILE : (half + 1) * TILE]).astype(BF16)
+        block = mm_tn(mixed[...], d_att_b[:, half * TILE : (half + 1) * TILE]).astype(BF16)
+        out_all[half] = block.reshape(4, 4, 4, 16, TILE)
     value_back(spread, d_mixed, values, normed_t, select, d_values, d_weights, put_value)
     score_back(scores, d_weights, d_scores)
     token_back(px, unit, inv, w_value, wq_high, d_values, d_scores, small)
     small[0:48, :] = mm_tn(d_scores[...], normed[...])[0:48, :]
     for q in range(LAT):
         small[136 + q : 137 + q, :] = jnp.sum(d_att[q * ROWS : (q + 1) * ROWS, :], axis=0, keepdims=True)
+    small_all[...] = small[...].astype(BF16).reshape(small_all.shape)
 
 
 def local_part(px, w_embed, level_embed, latents, w_query, w_key, w_value, w_out, w_up, w_down, cot):
@@ -242,11 +252,11 @@
         local_kernel,
         out_shape=(
             shape((pairs, width), BF16),
-            shape((ffn, width), BF16),
-            shape((ffn, width), BF16),
-            shape((2, inner, TILE), BF16),
-            shape((4, width, TILE), BF16),
-            shape((SMALL, width), F32),
+            shape((2, 4, 4, 4, 16, width), BF16),
+            shape((2, 4, 4, 4, 16, width), BF16),
+            shape((2, 4, 4, 4, 16, TILE), BF16),
+            shape((2, 4, 4, 4, 16, TILE), BF16),
+            shape((4, SMALL // 4, width), BF16),
         ),
         in_specs=[whole] * 11,
         out_specs=(whole,) * 6,
@@ -272,27 +282,285 @@
             pltpu.VMEM((every, inner), BF16),
             pltpu.VMEM((every, PAD), F32),
             pltpu.VMEM((every, PAD), BF16),
+            pltpu.VMEM((SMALL, width), F32),
         ],
         compiler_params=pltpu.CompilerParams(vmem_limit_bytes=60 * 1024 * 1024),
         name="local_part",
     )(px, w_embed, level_embed, latents, w_query, w_key, w_value, w_out, w_up, w_down, cot)
 
+MESH = pl.DeviceIdType.MESH
+SEMS = 112
+
+
+def place():
+    var, lon = lax.axis_index("var"), lax.axis_index("lon")
+    return {
+        "var": var,
+        "lon": lon,
+        "x": lon // 4,
+        "y": var % 4,
+        "z": (lon // 2) % 2 * 2 + var // 4,
+        "core": lon % 2,
+    }
+
+
+SIZES = {"x": 4, "y": 4, "z": 4, "core": 2, "var": 8}
+
+
+def peer(at, axis, index):
+    var, lon = at["var"], at["lon"]
+    if axis == "core":
+        return var, lon - at["core"] + index
+    if axis == "x":
+        return var, index * 4 + lon % 4
+    if axis == "y":
+        return var - at["y"] + index, lon
+    if axis == "z":
+        return (index % 2) * 4 + at["y"], at["x"] * 4 + (index // 2) * 2 + at["core"]
+    return index, lon
+
+
+def greet(at):
+    barrier = pltpu.get_barrier_semaphore()
+    others = [peer(at, "var", (at["var"] + d) % 8) for d in range(1, 8)]
+    others += [peer(at, "x", (at["x"] + d) % 4) for d in range(1, 4)]
+    others += [peer(at, "core", 1 - at["core"])]
+    far = (1 - at["z"] // 2) * 2
+    others += [peer(at, "z", far), peer(at, "z", far + 1)]
+    for other in others:
+        pl.semaphore_signal(barrier, inc=1, device_id=other, device_id_type=MESH)
+    pl.semaphore_wait(barrier, len(others))
+
+
+class Wires:
+    def __init__(self, at, send_sem, recv_sem):
+        self.at, self.send_sem, self.recv_sem, self.used = at, send_sem, recv_sem, 0
+
+    def copy(self, src, dst, device):
+        slot = self.used
+        self.used += 1
+        return pltpu.make_async_remote_copy(
+            src_ref=src,
+            dst_ref=dst,
+            send_sem=self.send_sem.at[slot],
+            recv_sem=self.recv_sem.at[slot],
+            device_id=device,
+            device_id_type=MESH,
+        )
+
+
+class Scatter:
+    def __init__(self, wires, axis, src, recv, out):
+        self.wires, self.axis, self.src, self.recv, self.out = wires, axis, src, recv, out
+
+    def start(self):
+        at, axis, size = self.wires.at, self.axis, SIZES[self.axis]
+        self.copies = []
+        for d in range(1, size):
+            to = (at[axis] + d) % size
+            copy = self.wires.copy(self.src.at[to], self.recv.at[d - 1], peer(at, axis, to))
+            copy.start()
+            self.copies.append(copy)
+
+    def finish(self):
+        for copy in self.copies:
+            copy.wait()
+        own, count = self.wires.at[self.axis], len(self.copies)
+
+        def add(index):
+            total = self.src[(own, *index)].astype(F32)
+            for d in range(count):
+                total = total + self.recv[(d, *index)].astype(F32)
+            self.out[index] = total.astype(BF16)
+
+        shape = self.out.shape
+        if math.prod(shape) > 65536:
+
+            @pl.loop(0, shape[0])
+            def _(i):
+                add((i,) + (slice(None),) * (len(shape) - 1))
+
+        else:
+            add((slice(None),) * len(shape))
+
+
+class Total:
+    def __init__(self, wires, axis, src, recv, out):
+        self.wires, self.axis, self.src, self.recv, self.out = wires, axis, src, recv, out
+
+    def start(self):
+        at, axis, size = self.wires.at, self.axis, SIZES[self.axis]
+        self.copies = []
+        for d in range(1, size):
+            to = (at[axis] + d) % size
+            copy = self.wires.copy(self.src, self.recv.at[d - 1], peer(at, axis, to))
+            copy.start()
+            self.copies.append(copy)
+
+    def finish(self):
+        for copy in self.copies:
+            copy.wait()
+        total = self.src[...].astype(F32)
+        for d in range(len(self.copies)):
+            total = total + self.recv[d].astype(F32)
+        self.out[...] = total.astype(BF16)
+
+
+class Gather:
+    def __init__(self, wires, axis, full):
+        self.wires, self.axis, self.full = wires, axis, full
+
+    def start(self):
+        at, axis, size = self.wires.at, self.axis, SIZES[self.axis]
+        own = self.full.at[at[axis]]
+        self.copies = []
+        for d in range(1, size):
+            copy = self.wires.copy(own, own, peer(at, axis, (at[axis] + d) % size))
+            copy.start()
+            self.copies.append(copy)
+
+    def finish(self):
+        for copy in self.copies:
+            copy.wait()
+
+
+class Chain:
+    def __init__(self, steps):
+        self.steps, self.next = steps, 0
+
+    def advance(self):
+        if self.next > 0:
+            self.steps[self.next - 1].finish()
+        if self.next < len(self.steps):
+            self.steps[self.next].start()
+        self.next += 1
+
+
+def spread_chain(wires, axes, src, recvs, sums, tail, last):
+    steps, block = [], src
+    for axis, recv, out in zip(("core", *axes), recvs, (*sums, last)):
+        steps.append(Scatter(wires, axis, block, recv, out))
+        block = out
+    return Chain(steps + tail)
+
+
+def whole_chain(wires, axes, src, recvs, sums, full):
+    at = wires.at
+    where = [at["core"], *(at[axis] for axis in axes)]
+    tail = [
+        Gather(wires, axis, full.at[tuple(where[:depth])] if depth else full)
+        for depth, axis in reversed(list(enumerate(("core", *axes))))
+    ]
+    return spread_chain(wires, axes, src, recvs, sums, tail, full.at[tuple(where)])
+
+
+def part_chain(wires, axes, src, recvs, sums, full):
+    last = full.at[wires.at["var"]]
+    return spread_chain(wires, axes, src, recvs, sums, [Gather(wires, "var", full)], last)
+
+
+def small_chain(wires, src, recvs, sums, full):
+    own = full.at[wires.at["y"]]
+    return Chain([
+        Total(wires, "core", src, recvs[0], sums[0]),
+        Scatter(wires, "y", sums[0], recvs[1], sums[1]),
+        Total(wires, "x", sums[1], recvs[2], sums[2]),
+        Total(wires, "z", sums[2], recvs[3], own),
+        Gather(wires, "y", full),
+    ])
+
+
+def chain_scratch(width):
+    block = (16, width)
+    recvs = [
+        pltpu.VMEM((1, 4, 4, 4, *block), BF16),
+        pltpu.VMEM((3, 4, 4, *block), BF16),
+        pltpu.VMEM((3, 4, *block), BF16),
+        pltpu.VMEM((3, *block), BF16),
+    ]
+    sums = [
+        pltpu.VMEM((4, 4, 4, *block), BF16),
+        pltpu.VMEM((4, 4, *block), BF16),
+        pltpu.VMEM((4, *block), BF16),
+    ]
+    return recvs, sums
+
+
+def small_scratch(width):
+    block = (SMALL // 4, width)
+    recvs = [
+        pltpu.VMEM((1, 4, *block), BF16),
+        pltpu.VMEM((3, *block), BF16),
+        pltpu.VMEM((3, *block), BF16),
+        pltpu.VMEM((3, *block), BF16),
+    ]
+    sums = [pltpu.VMEM((4, *block), BF16), pltpu.VMEM(block, BF16), pltpu.VMEM(block, BF16)]
+    return recvs, sums
+
+
+def sums_kernel(up, down, out, value, small, up_all, down_all, out_all, value_all, small_all, scratch, send_sem, recv_sem):
+    at = place()
+    greet(at)
+    wires = Wires(at, send_sem, recv_sem)
+    chains = [
+        part_chain(wires, ("y", "z", "x"), down, *scratch[0], down_all),
+        part_chain(wires, ("x", "y", "z"), up, *scratch[1], up_all),
+        whole_chain(wires, ("z", "x", "y"), out, *scratch[2], out_all),
+        whole_chain(wires, ("z", "x", "y"), value, *scratch[3], value_all),
+        small_chain(wires, small, *scratch[4], small_all),
+    ]
+    while any(chain.next <= len(chain.steps) for chain in chains):
+        for chain in chains:
+            if chain.next <= len(chain.steps):
+                chain.advance()
+
+
+def sums_part(up, down, out, value, small):
+    width = up.shape[-1]
+    shape = jax.ShapeDtypeStruct
+    whole = pl.BlockSpec(memory_space=pltpu.VMEM)
+    return pl.pallas_call(
+        sums_kernel,
+        out_shape=(
+            shape((8, 16, width), BF16),
+            shape((8, 16, width), BF16),
+            shape(out.shape, BF16),
+            shape(value.shape, BF16),
+            shape(small.shape, BF16),
+        ),
+        in_specs=[whole] * 5,
+        out_specs=(whole,) * 5,
+        scratch_shapes=[
+            [chain_scratch(width), chain_scratch(width), chain_scratch(TILE), chain_scratch(TILE), small_scratch(width)],
+            pltpu.SemaphoreType.DMA((SEMS,)),
+            pltpu.SemaphoreType.DMA((SEMS,)),
+        ],
+        compiler_params=pltpu.CompilerParams(
+            vmem_limit_bytes=60 * 1024 * 1024, collective_id=0, has_side_effects=True
+        ),
+        name="sums_part",
+    )(up, down, out, value, small)
+
 
 def finish_kernel(
-    small, value_all, out_all, latents, w_query, w_key,
-    grad_embed, grad_level, grad_lat, grad_query, grad_key, grad_value, grad_out,
+    small, value_all, out_all, up_part, down_part, latents, w_query, w_key,
+    grad_embed, grad_level, grad_lat, grad_query, grad_key, grad_value, grad_out, grad_up, grad_down,
 ):
-    grad_embed[...] = small[48:128, :].astype(F32)
-    grad_level[...] = small[128:136, :].astype(F32)
+    grad_up[...] = up_part[...].reshape(ROWS, -1).astype(F32).T
+    grad_down[...] = down_part[...].reshape(ROWS, -1).astype(F32)
+    rest = small[...].reshape(SMALL, -1)
+    grad_embed[...] = rest[48:128, :].astype(F32)
+    grad_level[...] = rest[128:136, :].astype(F32)
+    width, inner = w_key.shape
     for t in range(4):
-        grad_value[:, t * TILE : (t + 1) * TILE] = value_all[t].astype(F32)
+        block = value_all[t // 2, t % 2 * 2 : t % 2 * 2 + 2].reshape(width, TILE)
+        grad_value[:, t * TILE : (t + 1) * TILE] = block.astype(F32)
     for half in range(2):
-        grad_out[:, half * TILE : (half + 1) * TILE] = out_all[half].astype(F32)
+        grad_out[:, half * TILE : (half + 1) * TILE] = out_all[half].reshape(inner, TILE).astype(F32)
     rows = query_rows(latents[...], w_query[...])
-    high, low = split(small[0:48, :].astype(F32))
-    grad_key[...] = mm_tn(high, rows[0:48, :]) + mm_tn(low, rows[0:48, :])
-    spread = mm(high, w_key[...]) + mm(low, w_key[...])
-    inner = w_key.shape[1]
+    total = rest[0:48, :]
+    grad_key[...] = mm_tn(total, rows[0:48, :])
+    spread = mm(total, w_key[...])
     row = lax.broadcasted_iota(jnp.int32, (48, inner), 0)
     head = lax.broadcasted_iota(jnp.int32, (48, inner), 1) // HEAD
     own = []
@@ -301,10 +569,10 @@
     d_queries = jnp.concatenate(own, axis=0)
     high, low = split(d_queries)
     grad_query[...] = mm_tn(latents[...], high) + mm_tn(latents[...], low)
-    grad_lat[...] = small[136:139, :].astype(F32) + mm_nt(high, w_query[...]) + mm_nt(low, w_query[...])
-
-
-def finish(small, value_all, out_all, latents, w_query, w_key):
+    grad_lat[...] = rest[136:139, :].astype(F32) + mm_nt(high, w_query[...]) + mm_nt(low, w_query[...])
+
+
+def finish(small, value_all, out_all, up_part, down_part, latents, w_query, w_key):
     width, inner = w_key.shape
     shape = jax.ShapeDtypeStruct
     whole = pl.BlockSpec(memory_space=pltpu.VMEM)
@@ -318,12 +586,14 @@
             shape((width, inner), F32),
             shape((width, inner), F32),
             shape((inner, width), F32),
+            shape((width, ROWS), F32),
+            shape((ROWS, width), F32),
         ),
-        in_specs=[whole] * 6,
-        out_specs=(whole,) * 7,
+        in_specs=[whole] * 8,
+        out_specs=(whole,) * 9,
         compiler_params=pltpu.CompilerParams(vmem_limit_bytes=60 * 1024 * 1024),
         name="finish",
-    )(small, value_all, out_all, latents, w_query, w_key)
+    )(small, value_all, out_all, up_part, down_part, latents, w_query, w_key)
 
 
 def on_device(
@@ -337,15 +607,9 @@
         px, w_embed, level_embed, latents, w_query, w_key, w_value, w_out, w_up, w_down,
         cotangent.reshape(LAT * ROWS, width),
     )
-    both = jnp.concatenate(
-        [up_all.reshape(16, -1, width), down_all.reshape(16, -1, width)], axis=1
-    )
-    part = lax.psum_scatter(both, "lon", scatter_dimension=0, tiled=True)
-    part = lax.psum(part, "var")[0].astype(F32)
-    up_part, down_part = part[:ROWS], part[ROWS:]
-    small, value_all, out_all = lax.psum((small.astype(BF16), value_all, out_all), ("var", "lon"))
-    grads = finish(small, value_all, out_all, latents, w_query, w_key)
-    return (pooled.reshape(LAT, ROWS, width), *grads, jnp.transpose(up_part), down_part)
+    up_part, down_part, out_all, value_all, small = sums_part(up_all, down_all, out_all, value_all, small)
+    grads = finish(small, value_all, out_all, up_part, down_part, latents, w_query, w_key)
+    return (pooled.reshape(LAT, ROWS, width), *grads)
 
 
 def solution(mesh):

time: 318 us -> 120 us (0.38)
  waiting for transfers between devices: 235 us -> 0 us
  Pallas kernels: 44.3 us -> 104 us
  between operations: 15.5 us -> 0.66 us
  other arithmetic: 6.24 us -> 0 us
    psum x2 -> x0, waiting for transfers between devices: 156 us -> none  [the longest x1 89.1 us: on_device(): lax.psum((small.astype(BF16), value_all, out_all), ('var', 'lon'))]
    reduce_scatter x1 -> x0, waiting for transfers between devices: 79 us -> none  [on_device(): part = lax.psum_scatter(both, 'lon', scatter_dimension=0, tiled=True)]
    pallas_call x0 -> x1, Pallas kernels: none -> 60.5 us  [sums_part(): pl.pallas_call(sums_kernel, out_shape=(shape((8, 16, width), BF16), shape...]
    concatenate x1 -> x0, other arithmetic: 4.54 us -> none  [on_device(): jnp.concatenate([up_all.reshape(16, -1, width), down_all.reshape(16, -1,...]
  transfers between devices with their start and end apart: 3 -> 0, of which waited for: 3 -> 0; matrix products, arithmetic and copies ran while one was open for 0% -> 0% of each run, Pallas kernels for 2% -> 0%
where the time goes in v2:
time: 120 us; the launch traced here: 118 us
  Pallas kernels  104 us (87%)
  blocking collectives  12.6 us (10%)
    pallas_call x1, Pallas kernels, sums_part(): pl.pallas_call(sums_kernel, out_shape=(shape((8, 16, width), BF16), shape...  60.5 us
    pallas_call x1, Pallas kernels, local_part(): pl.pallas_call(local_kernel, out_shape=(shape((pairs, width), BF16), shap...  36.5 us
    all_to_all x1, blocking collectives, on_device(): px = lax.all_to_all(own, 'var', split_axis=1, concat_axis=1, tiled=True)  12.6 us
    pallas_call x1, Pallas kernels, finish(): pl.pallas_call(finish_kernel, out_shape=(shape((80, width), F32), shape((...  7.17 us

profile of v2, /device:TPU:0, one launch (start us, length us, event | category | flops | bytes accessed | tf_op | source)
XLA Modules:
  0.0 118.4 jit_solution(11600071343135339424)
XLA Ops:
  0.6 0.9 copy.22
  1.6 12.6 %all_to_all.5 = bf16[80,8,128]{2,0,1:T(8,128)(2,1)} all-to-all(bf16[80,8,128]{2,0,1:T(8,128)(2,1)S(1)} %copy.21), channel_id=1, replica_groups=mesh['var'=8,'lon'=16] {'var'}, dimensions={1} | all-to-all | bytes 327680 | tf_op jit(solution)/shard_map/all_to_all | solution.py:604
  14.2 36.5 %local_part.1 = (bf16[384,512]{1,0:T(8,128)(2,1)}, bf16[2,4,4,4,16,512]{5,4,3,2,1,0:T(8,128)(2,1)}, bf16[2,4,4,4,16,512]{5,4,3,2,1,0:T(8,128)(2,1)}, bf16[2,4,4,...) custom-call(bf16[8,80,128]{2,1,0:T(8,128)(2,1)} %bitcast.8, ...), custom_call_target="tpu_custom_call" | custom-call | tf_op jit(solution)/shard_map/local_part/pallas_call | solution.py:251
  50.7 60.5 %sums_part.1 = (bf16[8,16,512]{2,1,0:T(8,128)(2,1)}, bf16[8,16,512]{2,1,0:T(8,128)(2,1)}, bf16[2,4,4,4,16,256]{5,4,3,2,1,0:T(8,128)(2,1)}, bf16[2,4,4,4,16,256]{5,4,3,2,1,0:T(8,128)(2,1)}, bf16[4,48,512]{2,1,0:T(8,128)(2,1)}) custom-call(bf16[2,4,4,4,16,512]{5,4,3,2,1,0:T(8,128)(2,1)} %get-tuple-element.31.up, ...), custom_call_target="tpu_custom_call" | custom-call | tf_op jit(solution)/shard_map/sums_part/pallas_call | solution.py:522
  111.2 7.2 %finish.1 = (f32[80,512]{1,0:T(8,128)}, f32[8,512]{1,0:T(8,128)}, f32[3,512]{1,0:T(4,128)}, f32[512,1024]{1,0:T(8,128)}, f32[512,1024]{1,0:T(8,128)}, /*index=5*...) custom-call(bf16[4,48,512]{2,1,0:T(8,128)(2,1)} %get-tuple-element.36.small, ...), custom_call_target="tpu_custom_call" | custom-call | tf_op jit(solution)/shard_map/finish/pallas_call | solution.py:579
  (1 shorter events, 0.0 us)

commit v3 on v1

v3 whole, which is shorter than its diff:
```python
import functools
import math

import jax
import jax.numpy as jnp
from jax import lax
from jax.experimental import pallas as pl
from jax.experimental.pallas import tpu as pltpu
from jax.sharding import PartitionSpec as P

F32 = jnp.float32
BF16 = jnp.bfloat16
EPSILON = 1e-05
HEADS = 16
HEAD = 64
LEV = 8
LAT = 3
ROWS = 128
TILE = 256
PAD = 128
GELU_C = math.sqrt(2.0 / math.pi)
GELU_A = 0.044715


def mm(left, right):
    return lax.dot_general(left, right, (((1,), (0,)), ((), ())), preferred_element_type=F32)


def mm_nt(left, right):
    return lax.dot_general(left, right, (((1,), (1,)), ((), ())), preferred_element_type=F32)


def mm_tn(left, right):
    return lax.dot_general(left, right, (((0,), (0,)), ((), ())), preferred_element_type=F32)


def split(value):
    high = value.astype(BF16)
    return high, (value - high.astype(F32)).astype(BF16)


def head_rows(inner):
    row = lax.broadcasted_iota(jnp.int32, (PAD, inner), 0)
    head = lax.broadcasted_iota(jnp.int32, (PAD, inner), 1) // HEAD
    return row, head


def query_rows(latents, w_query):
    queries = mm(latents, w_query).astype(BF16).astype(F32)
    inner = queries.shape[1]
    row, head = head_rows(inner)
    spread = jnp.zeros((PAD, inner), F32)
    for q in range(LAT):
        spread = jnp.where(row == q * HEADS + head, queries[q : q + 1, :], spread)
    return spread.astype(BF16)


def prepare(latents, w_query, w_key, select, wq_high, wq_low):
    inner = w_key.shape[1]
    row, head = head_rows(inner)
    for q in range(LAT):
        select[q] = jnp.where(row == q * HEADS + head, 1.0, 0.0).astype(BF16)
    folded = mm_nt(query_rows(latents[...], w_query[...]), w_key[...])
    high, low = split(folded)
    wq_high[...] = high
    wq_low[...] = low


def forward(
    px, w_embed, level_embed, w_value, wq_high, wq_low, level_rows, unit, inv, normed, normed_t, values, scores
):
    level_rows[...] = level_embed[...].astype(F32)

    @pl.loop(0, LEV)
    def _(l):
        token = mm_tn(px[l].reshape(80, ROWS), w_embed[...]) + level_rows[pl.ds(l, 1), :]
        token = token.astype(BF16).astype(F32)
        center = token - jnp.mean(token, axis=-1, keepdims=True)
        inverse = lax.rsqrt(jnp.mean(center * center, axis=-1, keepdims=True) + EPSILON)
        own = center * inverse
        unit[l] = own
        inv[l] = jnp.broadcast_to(inverse, (ROWS, PAD))
        own = own.astype(BF16)
        normed[pl.ds(pl.multiple_of(l * ROWS, ROWS), ROWS), :] = own
        scores[l] = (mm_nt(own, wq_high[...]) + mm_nt(own, wq_low[...])) * (1.0 / math.sqrt(HEAD))
        values[l] = mm(own, w_value[...]).astype(BF16)

    normed_t[...] = normed[...].T


def softmax(scores, weights):
    highest = scores[0]
    for l in range(1, LEV):
        highest = jnp.maximum(highest, scores[l])
    total = jnp.zeros_like(highest)
    for l in range(LEV):
        expo = jnp.exp(scores[l] - highest)
        scores[l] = expo
        total = total + expo
    for l in range(LEV):
        prob = scores[l] / total
        scores[l] = prob
        weights[l * ROWS : (l + 1) * ROWS, :] = prob.astype(BF16)


def mix(weights, select, values, spread, mixed):
    inner = values.shape[2]

    @pl.loop(0, inner // TILE)
    def _(t):
        cols = pl.ds(pl.multiple_of(t * TILE, TILE), TILE)
        for q in range(LAT):
            total = jnp.zeros((ROWS, TILE), F32)
            for l in range(LEV):
                own = mm(weights[l * ROWS : (l + 1) * ROWS, :], select[q, :, cols])
                spread[q, l, :, cols] = own.astype(BF16)
                total = total + own * values[l, :, cols].astype(F32)
            mixed[q * ROWS : (q + 1) * ROWS, cols] = total.astype(BF16)


def attend(latents, mixed, w_out, attended):
    for q in range(LAT):
        rows = slice(q * ROWS, (q + 1) * ROWS)
        own = mm(mixed[rows, :], w_out[...]) + latents[q : q + 1, :].astype(F32)
        attended[rows, :] = own.astype(BF16)


def feed_forward(attended, cot, w_up, w_down, pool_sum, d_att, hidden, d_pre):
    pool_sum[...] = attended[...].astype(F32)
    d_att[...] = cot[...].astype(F32)

    @pl.loop(0, w_up.shape[1] // TILE)
    def _(t):
        cols = pl.ds(pl.multiple_of(t * TILE, TILE), TILE)
        pre = mm(attended[...], w_up[:, cols])
        square = pre * pre
        bent = jnp.tanh(GELU_C * (pre + GELU_A * (square * pre)))
        half = 0.5 * (1.0 + bent)
        own = (pre * half).astype(BF16)
        slope = half + 0.5 * pre * (1.0 - bent * bent) * (GELU_C * (1.0 + 3.0 * GELU_A * square))
        back = (mm_nt(cot[...], w_down[cols, :]) * slope).astype(BF16)
        hidden[:, cols] = own
        d_pre[:, cols] = back
        pool_sum[...] += mm(own, w_down[cols, :])
        d_att[...] += mm_nt(back, w_up[:, cols])


def value_grad(t, spread, d_mixed, normed_t, d_values):
    cols = slice(t * TILE, (t + 1) * TILE)
    for l in range(LEV):
        total = jnp.zeros((ROWS, TILE), F32)
        for q in range(LAT):
            d_mix = d_mixed[q * ROWS : (q + 1) * ROWS, cols].astype(F32)
            total = total + spread[q, l, :, cols].astype(F32) * d_mix
        d_values[l * ROWS : (l + 1) * ROWS, cols] = total.astype(BF16)
    return mm(normed_t[...], d_values[:, cols]).astype(BF16)


def weight_grad(d_mixed, values, select, d_weights):
    d_weights[...] = jnp.zeros_like(d_weights)

    @pl.loop(0, values.shape[2] // TILE)
    def _(t):
        cols = pl.ds(pl.multiple_of(t * TILE, TILE), TILE)
        for l in range(LEV):
            own = values[l, :, cols].astype(F32)
            back = jnp.zeros((ROWS, PAD), F32)
            for q in range(LAT):
                d_mix = d_mixed[q * ROWS : (q + 1) * ROWS, cols].astype(F32)
                back = back + mm_nt((d_mix * own).astype(BF16), select[q, :, cols])
            d_weights[l * ROWS : (l + 1) * ROWS, :] += back


def score_back(probs, d_weights, d_scores):
    total = jnp.zeros((ROWS, PAD), F32)
    for l in range(LEV):
        total = total + probs[l] * d_weights[l * ROWS : (l + 1) * ROWS, :]
    for l in range(LEV):
        rows = slice(l * ROWS, (l + 1) * ROWS)
        own = probs[l] * (d_weights[rows, :] - total) * (1.0 / math.sqrt(HEAD))
        d_scores[rows, :] = own.astype(BF16)


def token_back(levels, px, unit, inv, w_value, wq_high, d_values, d_scores, small, rest):
    for l in levels:
        rows = slice(l * ROWS, (l + 1) * ROWS)
        d_normed = mm_nt(d_values[rows, :], w_value[...]) + mm(d_scores[rows, :], wq_high[...])
        own = unit[l]
        inverse = inv[l][:, :1]
        d_token = inverse * (
            d_normed
            - jnp.mean(d_normed, axis=-1, keepdims=True)
            - own * jnp.mean(d_normed * own, axis=-1, keepdims=True)
        )
        d_token = d_token.astype(BF16)
        small[48:128, :] += mm(px[l].reshape(80, ROWS), d_token)
        rest[l : l + 1, :] = jnp.sum(d_token.astype(F32), axis=0, keepdims=True)


MESH = pl.DeviceIdType.MESH
SEMS = 176


def locate(var, lon):
    return {
        "var": var,
        "lon": lon,
        "x": lon // 4,
        "y": var % 4,
        "z": (lon // 2) % 2 * 2 + var // 4,
        "core": lon % 2,
    }


def place():
    return locate(lax.axis_index("var"), lax.axis_index("lon"))


SIZES = {"x": 4, "y": 4, "z": 4, "core": 2, "var": 8}


def peer(at, axis, index):
    var, lon = at["var"], at["lon"]
    if axis == "core":
        return var, lon - at["core"] + index
    if axis == "x":
        return var, index * 4 + lon % 4
    if axis == "y":
        return var - at["y"] + index, lon
    if axis == "z":
        return (index % 2) * 4 + at["y"], at["x"] * 4 + (index // 2) * 2 + at["core"]
    return index, lon


def greet(at):
    barrier = pltpu.get_barrier_semaphore()
    others = [peer(at, "core", 1 - at["core"])]
    steps = range(4)
    for i, j in [(i, j) for i in steps for j in steps if i or j]:
        along = locate(*peer(at, "y", (at["y"] + i) % 4))
        others.append(peer(along, "x", (at["x"] + j) % 4))
        if j:
            others.append(peer(along, "z", (at["z"] + j) % 4))
    for other in others:
        pl.semaphore_signal(barrier, inc=1, device_id=other, device_id_type=MESH)
    pl.semaphore_wait(barrier, len(others))


class Wires:
    def __init__(self, at, send_sem, recv_sem):
        self.at, self.send_sem, self.recv_sem, self.used = at, send_sem, recv_sem, 0

    def copy(self, src, dst, device):
        slot = self.used
        self.used += 1
        return pltpu.make_async_remote_copy(
            src_ref=src,
            dst_ref=dst,
            send_sem=self.send_sem.at[slot],
            recv_sem=self.recv_sem.at[slot],
            device_id=device,
            device_id_type=MESH,
        )


HOP = 2.7
LINK = 46e3
CHIP = 700e3


def size_of(ref):
    return 2 * math.prod(ref.shape)


def add_into(out, where, parts):
    total = parts[0][...].astype(F32)
    for part in parts[1:]:
        total = total + part[...].astype(F32)
    out[where] = total.astype(BF16)


class Step:
    def __init__(self, wires, axis):
        self.wires, self.axis, self.copies = wires, axis, []

    def send(self, src, dst, index):
        copy = self.wires.copy(src, dst, peer(self.wires.at, self.axis, index))
        copy.start()
        self.copies.append(copy)

    def others(self):
        own, size = self.wires.at[self.axis], SIZES[self.axis]
        return [(own + d) % size for d in range(1, size)]

    def cost(self, block):
        if self.axis == "core":
            return HOP / 2 + block / CHIP
        return HOP + block * {"x": 2, "y": 2, "z": 2, "var": 4}[self.axis] / LINK

    def wait(self):
        for copy in self.copies:
            copy.wait()


class Scatter(Step):
    def __init__(self, wires, axis, src, recv, out):
        super().__init__(wires, axis)
        self.src, self.recv, self.out = src, recv, out
        self.time = self.cost(size_of(out))

    def start(self):
        for d, to in enumerate(self.others()):
            self.send(self.src.at[to], self.recv.at[d], to)

    def finish(self):
        self.wait()
        own, count = self.wires.at[self.axis], len(self.copies)
        shape = self.out.shape

        def add(*index):
            refs = [self.src.at[own]] + [self.recv.at[d] for d in range(count)]
            where = index if index else (slice(None),) * len(shape)
            add_into(self.out, where, [ref.at[where] for ref in refs])

        if math.prod(shape) > 65536:

            @pl.loop(0, shape[0])
            def _(i):
                add(i, *((slice(None),) * (len(shape) - 1)))

        else:
            add()


class Total(Step):
    def __init__(self, wires, axis, src, recv, out):
        super().__init__(wires, axis)
        self.src, self.recv, self.out = src, recv, out
        self.time = self.cost(size_of(src))

    def start(self):
        for d, to in enumerate(self.others()):
            self.send(self.src, self.recv.at[d], to)

    def finish(self):
        self.wait()
        add_into(self.out, ..., [self.src] + [self.recv.at[d] for d in range(len(self.copies))])


class Gather(Step):
    def __init__(self, wires, axis, full):
        super().__init__(wires, axis)
        self.full = full
        self.time = self.cost(size_of(full) // full.shape[0])

    def start(self):
        own = self.full.at[self.wires.at[self.axis]]
        for to in self.others():
            self.send(own, own, to)

    def finish(self):
        self.wait()


class Plane(Step):
    def __init__(self, wires, axes):
        super().__init__(wires, axes)
        self.hop = HOP + 1.0

    def here(self):
        return tuple(self.wires.at[axis] for axis in self.axis)

    def others(self):
        first, second = self.here()
        ring = [(i, j) for i in range(4) for j in range(4) if i or j]
        return [((first + i) % 4, (second + j) % 4) for i, j in ring]

    def send(self, src, dst, index):
        at = dict(self.wires.at)
        for axis, place in zip(self.axis, index):
            var, lon = peer(at, axis, place)
            at = locate(var, lon)
        copy = self.wires.copy(src, dst, (var, lon))
        copy.start()
        self.copies.append(copy)


class PlaneScatter(Plane):
    def __init__(self, wires, axes, src, recv, out):
        super().__init__(wires, axes)
        self.src, self.recv, self.out = src, recv, out
        self.time = self.hop + size_of(out) * 8 / LINK

    def start(self):
        for d, to in enumerate(self.others()):
            self.send(self.src.at[to], self.recv.at[d], to)

    def finish(self):
        self.wait()
        parts = [self.src.at[self.here()]] + [self.recv.at[d] for d in range(15)]
        if len(self.out.shape) == 2:
            add_into(self.out, ..., parts)
        else:
            for k in range(self.out.shape[0]):
                add_into(self.out, (k,), [part.at[k] for part in parts])


class PlaneGather(Plane):
    def __init__(self, wires, axes, full):
        super().__init__(wires, axes)
        self.full = full
        self.time = self.hop + size_of(full) / 16 * 8 / LINK

    def start(self):
        own = self.full.at[self.here()]
        for to in self.others():
            self.send(own, own, to)

    def finish(self):
        self.wait()


def ring(at, axis):
    own = at[axis]
    return own, own + 1 - 2 * (own % 2), 3 - own, (own + 2) % 4


HALVES = (slice(0, 2), slice(2, 4))


class FoldFirst(Step):
    def __init__(self, wires, axis, src, recv, out):
        super().__init__(wires, axis)
        self.src, self.recv, self.out = src, recv, out
        self.time = HOP + size_of(out) / 2 / LINK

    def start(self):
        own, near, back, far = ring(self.wires.at, self.axis)
        for half, to in ((0, back), (1, near)):
            for slot, block in ((1, far), (0, to)):
                self.send(self.src.at[block, HALVES[half]], self.recv.at[half, slot], to)

    def finish(self):
        self.wait()
        own, near, back, far = ring(self.wires.at, self.axis)
        for half, other in ((0, near), (1, back)):
            for slot, block in ((1, other), (0, own)):
                for k in range(2):
                    add_into(
                        self.out,
                        (half, slot, k),
                        [self.src.at[block, 2 * half + k], self.recv.at[half, slot, k]],
                    )


class FoldSecond(Step):
    def __init__(self, wires, axis, src, recv, out):
        super().__init__(wires, axis)
        self.src, self.recv, self.out = src, recv, out
        self.time = HOP + size_of(out) / 2 / LINK

    def start(self):
        own, near, back, far = ring(self.wires.at, self.axis)
        for half, to in ((0, near), (1, back)):
            self.send(self.src.at[half, 1], self.recv.at[half], to)

    def finish(self):
        self.wait()
        for half in range(2):
            add_into(self.out, (HALVES[half],), [self.src.at[half, 0], self.recv.at[half]])


class Chain:
    def __init__(self, steps):
        self.steps, self.next = steps, 0

    def advance(self):
        if self.next > 0:
            self.steps[self.next - 1].finish()
        if self.next < len(self.steps):
            self.steps[self.next].start()
        self.next += 1


class Clock:
    def __init__(self):
        self.now, self.active = 0.0, []

    def begin(self, chain):
        chain.advance()
        chain.due = self.now + chain.steps[0].time
        self.active.append(chain)

    def step(self, chain):
        chain.advance()
        if chain.next > len(chain.steps):
            self.active.remove(chain)
        else:
            chain.due = max(self.now, chain.due) + chain.steps[chain.next - 1].time

    def passed(self, time):
        self.now += time
        for chain in sorted(self.active, key=lambda chain: chain.due):
            if chain.due <= self.now:
                self.step(chain)

    def drain(self):
        while self.active:
            chain = min(self.active, key=lambda chain: chain.due)
            self.now = max(self.now, chain.due)
            self.step(chain)


def spread_steps(wires, axes, src, recvs, sums, last):
    first, second, third = axes
    return [
        Scatter(wires, "core", src, recvs[0], sums[0]),
        FoldFirst(wires, first, sums[0], recvs[1], sums[1]),
        FoldSecond(wires, first, sums[1], recvs[2], sums[2]),
        Scatter(wires, second, sums[2], recvs[3], sums[3]),
        Scatter(wires, third, sums[3], recvs[4], last),
    ]


def whole_chain(wires, axes, src, recvs, sums, full):
    at = wires.at
    core, first, second, third = at["core"], *(at[axis] for axis in axes)
    return Chain([
        Scatter(wires, "core", src, recvs[0], sums[0]),
        PlaneScatter(wires, axes[:2], sums[0], recvs[1], sums[1]),
        Scatter(wires, axes[2], sums[1], recvs[2], full.at[core, first, second, third]),
        Gather(wires, axes[2], full.at[core, first, second]),
        PlaneGather(wires, axes[:2], full.at[core]),
        Gather(wires, "core", full),
    ])


def part_chain(wires, axes, src, recvs, sums, full):
    steps = spread_steps(wires, axes, src, recvs, sums, full.at[wires.at["var"]])
    return Chain(steps + [Gather(wires, "var", full)])


def small_chain(wires, src, recvs, sums, full):
    core, x, y = wires.at["core"], wires.at["x"], wires.at["y"]
    return Chain([
        Scatter(wires, "core", src, recvs[0], sums[0]),
        PlaneScatter(wires, ("x", "y"), sums[0], recvs[1], sums[1]),
        Total(wires, "z", sums[1], recvs[2], full.at[core, x, y]),
        PlaneGather(wires, ("x", "y"), full.at[core]),
        Gather(wires, "core", full),
    ])


def chain_scratch(width):
    block = (16, width)
    recvs = [
        pltpu.VMEM((1, 4, 4, 4, *block), BF16),
        pltpu.VMEM((2, 2, 2, 4, *block), BF16),
        pltpu.VMEM((2, 2, 4, *block), BF16),
        pltpu.VMEM((3, 4, *block), BF16),
        pltpu.VMEM((3, *block), BF16),
    ]
    sums = [
        pltpu.VMEM((4, 4, 4, *block), BF16),
        pltpu.VMEM((2, 2, 2, 4, *block), BF16),
        pltpu.VMEM((4, 4, *block), BF16),
        pltpu.VMEM((4, *block), BF16),
    ]
    return recvs, sums


def whole_scratch(width):
    block = (16, width)
    recvs = [
        pltpu.VMEM((1, 4, 4, 4, *block), BF16),
        pltpu.VMEM((15, 4, *block), BF16),
        pltpu.VMEM((3, *block), BF16),
    ]
    sums = [pltpu.VMEM((4, 4, 4, *block), BF16), pltpu.VMEM((4, *block), BF16)]
    return recvs, sums


SMALL_SHAPE = (2, 4, 4, 16, TILE)


def small_scratch():
    block = SMALL_SHAPE[3:]
    recvs = [
        pltpu.VMEM((1, 4, 4, *block), BF16),
        pltpu.VMEM((15, *block), BF16),
        pltpu.VMEM((3, *block), BF16),
    ]
    sums = [pltpu.VMEM((4, 4, *block), BF16), pltpu.VMEM(block, BF16)]
    return recvs, sums


def chain_shapes(width):
    return (2, 4, 4, 4, 16, width)


WEIGHTS = 10


def main_kernel(
    pixels, w_embed_h, level_embed_h, latents_h, w_query_h, w_key_h, w_value_h, w_out_h, w_up_h, w_down_h, cot_h,
    pooled, up_all, down_all, out_all, value_all, small_all,
    loaded, work, grads, scratch, load_sem, send_sem, recv_sem,
):
    w_embed, level_embed, latents, w_query, w_key, w_value, w_out, w_up, w_down, cot, px = loaded
    (
        select, wq_high, wq_low, level_rows, unit, inv, normed, normed_t, values, scores, weights, spread, mixed,
        attended, pool_sum, d_att, d_att_b, d_mixed, d_values, d_weights, d_scores, hidden, d_pre, small, rest,
    ) = work
    up, down, out, value, small_b = grads
    at = place()
    wires = Wires(at, send_sem, recv_sem)

    pairs = [
        (latents_h, latents), (w_query_h, w_query), (w_key_h, w_key), (w_embed_h, w_embed),
        (level_embed_h, level_embed), (w_value_h, w_value), (w_out_h, w_out), (cot_h, cot),
        (w_up_h, w_up), (w_down_h, w_down),
    ]
    loads = [pltpu.make_async_copy(src, dst, load_sem.at[i]) for i, (src, dst) in enumerate(pairs)]
    for load in loads:
        load.start()

    def patches(index):
        return pixels.at[:, :, pl.ds(pl.multiple_of(index * ROWS, ROWS), ROWS)]

    keep = pltpu.make_async_copy(patches(at["var"]), px.at[at["var"]], load_sem.at[WEIGHTS])
    keep.start()
    greet(at)
    moves = []
    for d in range(1, 8):
        to = (at["var"] + d) % 8
        move = wires.copy(patches(to), px.at[at["var"]], peer(at, "var", to))
        move.start()
        moves.append(move)

    for load in loads[:3]:
        load.wait()
    prepare(latents, w_query, w_key, select, wq_high, wq_low)
    for load in loads[3:6]:
        load.wait()
    keep.wait()
    for move in moves:
        move.wait()
    forward(
        px, w_embed, level_embed, w_value, wq_high, wq_low, level_rows, unit, inv, normed, normed_t, values, scores
    )
    softmax(scores, weights)
    mix(weights, select, values, spread, mixed)
    for load in loads[6:]:
        load.wait()
    attend(latents, mixed, w_out, attended)

    chain_down = part_chain(wires, ("z", "x", "y"), down, *scratch[0], down_all)
    chain_up = part_chain(wires, ("x", "z", "y"), up, *scratch[1], up_all)
    chain_out = whole_chain(wires, ("x", "y", "z"), out, *scratch[2], out_all)
    chain_value = whole_chain(wires, ("y", "z", "x"), value, *scratch[3], value_all)
    chain_small = small_chain(wires, small_b, *scratch[4], small_all)
    clock = Clock()

    feed_forward(attended, cot, w_up, w_down, pool_sum, d_att, hidden, d_pre)
    d_att_b[...] = d_att[...].astype(BF16)
    for half in range(2):
        block = mm_tn(mixed[...], d_att_b[:, half * TILE : (half + 1) * TILE]).astype(BF16)
        out[half] = block.reshape(4, 4, 4, 16, TILE)
    clock.begin(chain_out)
    d_mixed[...] = mm_nt(d_att_b[...], w_out[...]).astype(BF16)
    clock.passed(0.8)
    for t in range(4):
        block = value_grad(t, spread, d_mixed, normed_t, d_values)
        value[t // 2, t % 2 * 2 : t % 2 * 2 + 2] = block.reshape(2, 4, 4, 16, TILE)
        clock.passed(0.7)
    clock.begin(chain_value)

    for t in range(8):
        cols = slice(t * TILE, (t + 1) * TILE)
        block = mm_tn(hidden[:, cols], cot[...]).astype(BF16)
        for core in range(2):
            for var in range(8):
                start = core * 128 + var * 16
                down[core, t % 2 * 2 + var // 4, t // 2, var % 4] = block[start : start + 16]
        clock.passed(0.25)
    clock.begin(chain_down)
    for t in range(8):
        cols = slice(t * TILE, (t + 1) * TILE)
        block = mm_tn(d_pre[:, cols], attended[...]).astype(BF16)
        for core in range(2):
            for var in range(8):
                start = core * 128 + var * 16
                up[core, t // 2, t % 2 * 2 + var // 4, var % 4] = block[start : start + 16]
        clock.passed(0.25)
    clock.begin(chain_up)

    weight_grad(d_mixed, values, select, d_weights)
    clock.passed(2.5)
    score_back(scores, d_weights, d_scores)
    pooled[...] = pool_sum[...].astype(BF16)
    clock.passed(0.5)
    small[...] = jnp.zeros_like(small)
    rest[...] = jnp.zeros_like(rest)
    for l in range(0, LEV, 2):
        token_back((l, l + 1), px, unit, inv, w_value, wq_high, d_values, d_scores, small, rest)
        clock.passed(1.7)
    small[0:48, :] = mm_tn(d_scores[...], normed[...])[0:48, :]
    for q in range(LAT):
        rest[8 + q : 9 + q, :] = jnp.sum(d_att[q * ROWS : (q + 1) * ROWS, :], axis=0, keepdims=True)
    small_b[...] = jnp.zeros_like(small_b)
    for k in range(2):
        cols = slice(k * TILE, (k + 1) * TILE)
        small_b[0, 2 * k : 2 * k + 2] = small[:, cols].astype(BF16).reshape(2, 4, 16, TILE)
        small_b[1, 0, k] = rest[:, cols].astype(BF16)
    clock.passed(0.5)
    clock.begin(chain_small)
    clock.drain()


def main_part(pixels, w_embed, level_embed, latents, w_query, w_key, w_value, w_out, w_up, w_down, cot):
    width, inner = w_key.shape
    every, pairs = LEV * ROWS, LAT * ROWS
    shape = jax.ShapeDtypeStruct
    whole = pl.BlockSpec(memory_space=pltpu.VMEM)
    vmem = pltpu.VMEM
    arrays = (w_embed, level_embed, latents, w_query, w_key, w_value, w_out, w_up, w_down, cot)
    loaded = [vmem(array.shape, BF16) for array in arrays] + [vmem((LEV, 5, 16, ROWS), BF16)]
    work = [
        vmem((LAT, PAD, inner), BF16),
        vmem((PAD, width), BF16),
        vmem((PAD, width), BF16),
        vmem((LEV, width), F32),
        vmem((LEV, ROWS, width), F32),
        vmem((LEV, ROWS, PAD), F32),
        vmem((every, width), BF16),
        vmem((width, every), BF16),
        vmem((LEV, ROWS, inner), BF16),
        vmem((LEV, ROWS, PAD), F32),
        vmem((every, PAD), BF16),
        vmem((LAT, LEV, ROWS, inner), BF16),
        vmem((pairs, inner), BF16),
        vmem((pairs, width), BF16),
        vmem((pairs, width), F32),
        vmem((pairs, width), F32),
        vmem((pairs, width), BF16),
        vmem((pairs, inner), BF16),
        vmem((every, inner), BF16),
        vmem((every, PAD), F32),
        vmem((every, PAD), BF16),
        vmem((pairs, w_up.shape[1]), BF16),
        vmem((pairs, w_up.shape[1]), BF16),
        vmem((128, width), F32),
        vmem((16, width), F32),
    ]
    grads = [
        vmem(chain_shapes(width), BF16),
        vmem(chain_shapes(width), BF16),
        vmem(chain_shapes(TILE), BF16),
        vmem(chain_shapes(TILE), BF16),
        vmem(SMALL_SHAPE, BF16),
    ]
    return pl.pallas_call(
        main_kernel,
        out_shape=(
            shape((pairs, width), BF16),
            shape((8, 16, width), BF16),
            shape((8, 16, width), BF16),
            shape(chain_shapes(TILE), BF16),
            shape(chain_shapes(TILE), BF16),
            shape(SMALL_SHAPE, BF16),
        ),
        in_specs=[pl.BlockSpec(memory_space=pl.ANY)] * 11,
        out_specs=(whole,) * 6,
        scratch_shapes=[
            loaded,
            work,
            grads,
            [chain_scratch(width), chain_scratch(width), whole_scratch(TILE), whole_scratch(TILE), small_scratch()],
            pltpu.SemaphoreType.DMA((WEIGHTS + 1,)),
            pltpu.SemaphoreType.DMA((SEMS,)),
            pltpu.SemaphoreType.DMA((SEMS,)),
        ],
        compiler_params=pltpu.CompilerParams(
            vmem_limit_bytes=60 * 1024 * 1024, collective_id=0, has_side_effects=True
        ),
        name="main_part",
    )(pixels, w_embed, level_embed, latents, w_query, w_key, w_value, w_out, w_up, w_down, cot)


def finish_kernel(
    small_h, value_h, out_h, up_h, down_h, latents, w_query_h, w_key_h,
    grad_embed, grad_level, grad_lat, grad_up, grad_down, query_h, key_h, value_g, out_g,
    small, value_all, out_all, w_query, w_key, grad_query, grad_key, grad_value, grad_out, up_part, down_part,
    load_sem, save_sem,
):
    pairs = [
        (value_h, value_all), (out_h, out_all), (small_h, small), (w_query_h, w_query), (w_key_h, w_key),
        (up_h, up_part), (down_h, down_part),
    ]
    loads = [pltpu.make_async_copy(src, dst, load_sem.at[i]) for i, (src, dst) in enumerate(pairs)]
    for load in loads:
        load.start()
    saves = []

    def save(src, dst):
        copy = pltpu.make_async_copy(src, dst, save_sem.at[len(saves)])
        copy.start()
        saves.append(copy)

    width, inner = w_key.shape
    loads[0].wait()
    for t in range(4):
        block = value_all[t // 2, t % 2 * 2 : t % 2 * 2 + 2].reshape(width, TILE)
        cols = slice(t * TILE, (t + 1) * TILE)
        grad_value[:, cols] = block.astype(F32)
        save(grad_value.at[:, cols], value_g.at[:, cols])
    loads[1].wait()
    for half in range(2):
        cols = slice(half * TILE, (half + 1) * TILE)
        grad_out[:, cols] = out_all[half].reshape(inner, TILE).astype(F32)
        save(grad_out.at[:, cols], out_g.at[:, cols])
    for load in loads[2:5]:
        load.wait()
    sums = jnp.concatenate([small[0, 2 * k : 2 * k + 2].reshape(128, TILE) for k in range(2)], axis=1)
    rest = jnp.concatenate([small[1, 0, k] for k in range(2)], axis=1)
    total = sums[0:48, :]
    rows = query_rows(latents[...], w_query[...])
    for t in range(2):
        cols = slice(t * 512, (t + 1) * 512)
        grad_key[:, cols] = mm_tn(total, rows[0:48, cols])
        save(grad_key.at[:, cols], key_h.at[:, cols])
    spread = mm(total, w_key[...])
    row = lax.broadcasted_iota(jnp.int32, (48, inner), 0)
    head = lax.broadcasted_iota(jnp.int32, (48, inner), 1) // HEAD
    own = []
    for q in range(LAT):
        own.append(jnp.sum(jnp.where(row == q * HEADS + head, spread, 0.0), axis=0, keepdims=True))
    d_queries = jnp.concatenate(own, axis=0)
    high, low = split(d_queries)
    for t in range(2):
        cols = slice(t * 512, (t + 1) * 512)
        grad_query[:, cols] = mm_tn(latents[...], high[:, cols]) + mm_tn(latents[...], low[:, cols])
        save(grad_query.at[:, cols], query_h.at[:, cols])
    grad_lat[...] = rest[8:11, :].astype(F32) + mm_nt(high, w_query[...]) + mm_nt(low, w_query[...])
    grad_embed[...] = sums[48:128, :].astype(F32)
    grad_level[...] = rest[0:8, :].astype(F32)
    for load in loads[5:]:
        load.wait()
    grad_up[...] = up_part[...].reshape(ROWS, -1).astype(F32).T
    grad_down[...] = down_part[...].reshape(ROWS, -1).astype(F32)
    for copy in saves:
        copy.wait()


def finish(small, value_all, out_all, up_part, down_part, latents, w_query, w_key):
    width, inner = w_key.shape
    shape = jax.ShapeDtypeStruct
    whole = pl.BlockSpec(memory_space=pltpu.VMEM)
    anywhere = pl.BlockSpec(memory_space=pl.ANY)
    vmem = pltpu.VMEM
    embed, level, lat, up, down, query, key, value, out = pl.pallas_call(
        finish_kernel,
        out_shape=(
            shape((80, width), F32),
            shape((LEV, width), F32),
            shape((LAT, width), F32),
            shape((width, ROWS), F32),
            shape((ROWS, width), F32),
            shape((width, inner), F32),
            shape((width, inner), F32),
            shape((width, inner), F32),
            shape((inner, width), F32),
        ),
        in_specs=[anywhere] * 5 + [whole] + [anywhere] * 2,
        out_specs=(whole,) * 5 + (anywhere,) * 4,
        scratch_shapes=[
            vmem(small.shape, BF16),
            vmem(value_all.shape, BF16),
            vmem(out_all.shape, BF16),
            vmem(w_query.shape, BF16),
            vmem(w_key.shape, BF16),
            vmem((width, inner), F32),
            vmem((width, inner), F32),
            vmem((width, inner), F32),
            vmem((inner, width), F32),
            vmem(up_part.shape, BF16),
            vmem(down_part.shape, BF16),
            pltpu.SemaphoreType.DMA((7,)),
            pltpu.SemaphoreType.DMA((10,)),
        ],
        compiler_params=pltpu.CompilerParams(vmem_limit_bytes=60 * 1024 * 1024),
        name="finish",
    )(small, value_all, out_all, up_part, down_part, latents, w_query, w_key)
    return embed, level, lat, query, key, value, out, up, down


def on_device(
    pixels, w_embed, level_embed, latents, w_query, w_key, w_value, w_out, w_up, w_down, cotangent
):
    width = w_embed.shape[1]
    pooled, up_part, down_part, out_all, value_all, small = main_part(
        pixels[0], w_embed, level_embed, latents, w_query, w_key, w_value, w_out, w_up, w_down,
        cotangent.reshape(LAT * ROWS, width),
    )
    grads = finish(small, value_all, out_all, up_part, down_part, latents, w_query, w_key)
    return (pooled.reshape(LAT, ROWS, width), *grads)


def solution(mesh):
    return jax.shard_map(
        on_device,
        mesh=mesh,
        in_specs=(
            P("var", None, None, "lon"),
            *([P()] * 9),
            P(None, ("lon", "var"), None),
        ),
        out_specs=(
            P(None, ("lon", "var"), None),
            *([P()] * 7),
            P(None, "lon"),
            P("lon", None),
        ),
        check_vma=False,
    )
```

time: 318 us -> 96.6 us (0.30)
  waiting for transfers between devices: 235 us -> 0 us
  Pallas kernels: 44.3 us -> 95 us
  between operations: 15.5 us -> 0.68 us
  blocking collectives: 12.6 us -> 0 us
  other arithmetic: 6.24 us -> 0 us
    psum x2 -> x0, waiting for transfers between devices: 156 us -> none  [the longest x1 89.1 us: on_device(): lax.psum((small.astype(BF16), value_all, out_all), ('var', 'lon'))]
    reduce_scatter x1 -> x0, waiting for transfers between devices: 79 us -> none  [on_device(): part = lax.psum_scatter(both, 'lon', scatter_dimension=0, tiled=True)]
    pallas_call x1, Pallas kernels: 36.5 us -> 88.5 us  [main_part(): pl.pallas_call(main_kernel, out_shape=(shape((pairs, width), BF16), shape...]
    all_to_all x1 -> x0, blocking collectives: 12.6 us -> none  [on_device(): px = lax.all_to_all(own, 'var', split_axis=1, concat_axis=1, tiled=True)]
    concatenate x1 -> x0, other arithmetic: 4.54 us -> none  [on_device(): jnp.concatenate([up_all.reshape(16, -1, width), down_all.reshape(16, -1,...]
  transfers between devices with their start and end apart: 3 -> 0, of which waited for: 3 -> 0; matrix products, arithmetic and copies ran while one was open for 0% -> 0% of each run, Pallas kernels for 2% -> 0%
where the time goes in v3:
time: 96.6 us; the launch traced here: 96.5 us
  Pallas kernels  95 us (98%)
    pallas_call x1, Pallas kernels, main_part(): pl.pallas_call(main_kernel, out_shape=(shape((pairs, width), BF16), shape...  88.5 us
    pallas_call x1, Pallas kernels, finish(): pl.pallas_call(finish_kernel, out_shape=(shape((80, width), F32), shape((...  6.54 us

profile of v3, /device:TPU:0, one launch (start us, length us, event | category | flops | bytes accessed | tf_op | source)
XLA Modules:
  0.0 96.5 jit_solution(11000221484046214266)
XLA Ops:
  0.6 88.5 %main_part.1 = (bf16[384,512]{1,0:T(8,128)(2,1)}, bf16[8,16,512]{2,1,0:T(8,128)(2,1)}, bf16[8,16,512]{2,1,0:T(8,128)(2,1)}, bf16[2,4,4,4,16,256]{5,4,3,2,1,0:T(8...) custom-call(bf16[5,16,1024]{2,1,0:T(8,128)(2,1)} %bitcast.5, ...), custom_call_target="tpu_custom_call" | custom-call | tf_op jit(solution)/shard_map/main_part/pallas_call | solution.py:762
  89.1 0.0 copy-start
  89.1 6.5 %finish.1 = (f32[80,512]{1,0:T(8,128)}, f32[8,512]{1,0:T(8,128)}, f32[3,512]{1,0:T(4,128)}, f32[512,128]{1,0:T(8,128)}, f32[128,512]{1,0:T(8,128)}, /*index=5*/f...) custom-call(bf16[2,4,4,16,256]{4,3,2,1,0:T(8,128)(2,1)} %get-tuple-element.26.small_h, ...), custom_call_target="tpu_custom_call" | custom-call | tf_op jit(solution)/shard_map/finish/pallas_call | solution.py:861
  95.7 0.0 copy-done
  95.7 0.7 copy.22
Async XLA Ops:
  89.1 6.6 %copy-start = (bf16[384,512]{1,0:T(8,128)(2,1)S(1)}, bf16[384,512]{1,0:T(8,128)(2,1)}, u32[]{:S(2)}) copy-start(bf16[384,512]{1,0:T(8,128)(2,1)} %get-tuple-element.25) | copy-start | bytes 1179652

commit v4 on v3

--- a/solution.py
+++ b/solution.py
@@ -55,12 +55,29 @@
     return spread.astype(BF16)
 
 
-def prepare(latents, w_query, w_key, select, wq_high, wq_low):
+def query_back(small_all, w_query, w_key, d_queries, d_lat):
+    inner = w_key.shape[1]
+    total = jnp.concatenate([small_all[0, 2 * k, 0:3].reshape(48, TILE) for k in range(2)], axis=1)
+    rest = jnp.concatenate([small_all[1, 0, k] for k in range(2)], axis=1)
+    spread = mm(total, w_key[...])
+    row = lax.broadcasted_iota(jnp.int32, (48, inner), 0)
+    head = lax.broadcasted_iota(jnp.int32, (48, inner), 1) // HEAD
+    d_queries[...] = jnp.zeros_like(d_queries)
+    for q in range(LAT):
+        own = jnp.where(row == q * HEADS + head, spread, 0.0)
+        d_queries[q : q + 1, :] = jnp.sum(own, axis=0, keepdims=True)
+    high, low = split(d_queries[...])
+    d_lat[...] = mm_nt(high, w_query[...]) + mm_nt(low, w_query[...]) + rest[8:16, :].astype(F32)
+
+
+def prepare(latents, w_query, w_key, select, wq_high, wq_low, rows):
     inner = w_key.shape[1]
     row, head = head_rows(inner)
     for q in range(LAT):
         select[q] = jnp.where(row == q * HEADS + head, 1.0, 0.0).astype(BF16)
-    folded = mm_nt(query_rows(latents[...], w_query[...]), w_key[...])
+    spread = query_rows(latents[...], w_query[...])
+    rows[...] = spread[0:48, :]
+    folded = mm_nt(spread, w_key[...])
     high, low = split(folded)
     wq_high[...] = high
     wq_low[...] = low
@@ -71,7 +88,7 @@
 ):
     level_rows[...] = level_embed[...].astype(F32)
 
-    @pl.loop(0, LEV)
+    @pl.loop(0, LEV, unroll=2)
     def _(l):
         token = mm_tn(px[l].reshape(80, ROWS), w_embed[...]) + level_rows[pl.ds(l, 1), :]
         token = token.astype(BF16).astype(F32)
@@ -81,11 +98,11 @@
         unit[l] = own
         inv[l] = jnp.broadcast_to(inverse, (ROWS, PAD))
         own = own.astype(BF16)
-        normed[pl.ds(pl.multiple_of(l * ROWS, ROWS), ROWS), :] = own
+        rows = pl.ds(pl.multiple_of(l * ROWS, ROWS), ROWS)
+        normed[rows, :] = own
+        normed_t[:, rows] = own.T
         scores[l] = (mm_nt(own, wq_high[...]) + mm_nt(own, wq_low[...])) * (1.0 / math.sqrt(HEAD))
         values[l] = mm(own, w_value[...]).astype(BF16)
-
-    normed_t[...] = normed[...].T
 
 
 def softmax(scores, weights):
@@ -125,34 +142,33 @@
         attended[rows, :] = own.astype(BF16)
 
 
-def feed_forward(attended, cot, w_up, w_down, pool_sum, d_att, hidden, d_pre):
-    pool_sum[...] = attended[...].astype(F32)
+def feed_forward(attended, cot, w_up, d_hidden, d_att, hidden, d_pre):
     d_att[...] = cot[...].astype(F32)
 
-    @pl.loop(0, w_up.shape[1] // TILE)
+    @pl.loop(0, w_up.shape[1] // TILE, unroll=2)
     def _(t):
         cols = pl.ds(pl.multiple_of(t * TILE, TILE), TILE)
         pre = mm(attended[...], w_up[:, cols])
         square = pre * pre
-        bent = jnp.tanh(GELU_C * (pre + GELU_A * (square * pre)))
-        half = 0.5 * (1.0 + bent)
-        own = (pre * half).astype(BF16)
-        slope = half + 0.5 * pre * (1.0 - bent * bent) * (GELU_C * (1.0 + 3.0 * GELU_A * square))
-        back = (mm_nt(cot[...], w_down[cols, :]) * slope).astype(BF16)
+        bent = jnp.tanh(pre * (GELU_C + GELU_C * GELU_A * square))
+        half = 0.5 + 0.5 * bent
+        out = pre * half
+        own = out.astype(BF16)
+        slope = half + out * (1.0 - bent) * (GELU_C + 3.0 * GELU_C * GELU_A * square)
+        back = (d_hidden[:, cols] * slope).astype(BF16)
         hidden[:, cols] = own
         d_pre[:, cols] = back
-        pool_sum[...] += mm(own, w_down[cols, :])
         d_att[...] += mm_nt(back, w_up[:, cols])
 
 
 def value_grad(t, spread, d_mixed, normed_t, d_values):
     cols = slice(t * TILE, (t + 1) * TILE)
     for l in range(LEV):
-        total = jnp.zeros((ROWS, TILE), F32)
+        total = None
         for q in range(LAT):
-            d_mix = d_mixed[q * ROWS : (q + 1) * ROWS, cols].astype(F32)
-            total = total + spread[q, l, :, cols].astype(F32) * d_mix
-        d_values[l * ROWS : (l + 1) * ROWS, cols] = total.astype(BF16)
+            own = spread[q, l, :, cols] * d_mixed[q * ROWS : (q + 1) * ROWS, cols]
+            total = own if total is None else total + own
+        d_values[l * ROWS : (l + 1) * ROWS, cols] = total
     return mm(normed_t[...], d_values[:, cols]).astype(BF16)
 
 
@@ -163,11 +179,11 @@
     def _(t):
         cols = pl.ds(pl.multiple_of(t * TILE, TILE), TILE)
         for l in range(LEV):
-            own = values[l, :, cols].astype(F32)
+            own = values[l, :, cols]
             back = jnp.zeros((ROWS, PAD), F32)
             for q in range(LAT):
-                d_mix = d_mixed[q * ROWS : (q + 1) * ROWS, cols].astype(F32)
-                back = back + mm_nt((d_mix * own).astype(BF16), select[q, :, cols])
+                d_mix = d_mixed[q * ROWS : (q + 1) * ROWS, cols]
+                back = back + mm_nt(d_mix * own, select[q, :, cols])
             d_weights[l * ROWS : (l + 1) * ROWS, :] += back
 
 
@@ -198,7 +214,7 @@
 
 
 MESH = pl.DeviceIdType.MESH
-SEMS = 176
+SEMS = 160
 
 
 def locate(var, lon):
@@ -239,8 +255,9 @@
     for i, j in [(i, j) for i in steps for j in steps if i or j]:
         along = locate(*peer(at, "y", (at["y"] + i) % 4))
         others.append(peer(along, "x", (at["x"] + j) % 4))
-        if j:
-            others.append(peer(along, "z", (at["z"] + j) % 4))
+    others += [peer(at, "z", (at["z"] + i) % 4) for i in (1, 2, 3)]
+    across = locate(*peer(at, "z", at["z"] + 1 - at["z"] % 2 * 2))
+    others += [peer(across, "y", (at["y"] + i) % 4) for i in (1, 2, 3)]
     for other in others:
         pl.semaphore_signal(barrier, inc=1, device_id=other, device_id_type=MESH)
     pl.semaphore_wait(barrier, len(others))
@@ -265,7 +282,8 @@
 
 HOP = 2.7
 LINK = 46e3
-CHIP = 700e3
+CHIP = 500e3
+ADD = 1.5 / 1024 / 2200
 
 
 def size_of(ref):
@@ -273,6 +291,9 @@
 
 
 def add_into(out, where, parts):
+    if len(parts) == 2:
+        out[where] = parts[0][...] + parts[1][...]
+        return
     total = parts[0][...].astype(F32)
     for part in parts[1:]:
         total = total + part[...].astype(F32)
@@ -282,6 +303,7 @@
 class Step:
     def __init__(self, wires, axis):
         self.wires, self.axis, self.copies = wires, axis, []
+        self.hop, self.load, self.work = HOP, {}, 0.0
 
     def send(self, src, dst, index):
         copy = self.wires.copy(src, dst, peer(self.wires.at, self.axis, index))
@@ -292,10 +314,16 @@
         own, size = self.wires.at[self.axis], SIZES[self.axis]
         return [(own + d) % size for d in range(1, size)]
 
-    def cost(self, block):
+    def cost(self, block, parts=0):
+        self.work = block / 2 * (parts + 1) * ADD if parts else 0.0
         if self.axis == "core":
-            return HOP / 2 + block / CHIP
-        return HOP + block * {"x": 2, "y": 2, "z": 2, "var": 4}[self.axis] / LINK
+            self.hop, self.load = HOP / 2, {"core": block / CHIP}
+        elif self.axis == "var":
+            self.load = {"y": 4 * block / LINK, "z": 4 * block / LINK}
+        elif isinstance(self.axis, tuple):
+            self.hop, self.load = HOP + 1.0, {axis: 8 * block / LINK for axis in self.axis}
+        else:
+            self.load = {self.axis: 2 * block / LINK}
 
     def wait(self):
         for copy in self.copies:
@@ -306,7 +334,7 @@
     def __init__(self, wires, axis, src, recv, out):
         super().__init__(wires, axis)
         self.src, self.recv, self.out = src, recv, out
-        self.time = self.cost(size_of(out))
+        self.cost(size_of(out), SIZES[axis])
 
     def start(self):
         for d, to in enumerate(self.others()):
@@ -336,7 +364,7 @@
     def __init__(self, wires, axis, src, recv, out):
         super().__init__(wires, axis)
         self.src, self.recv, self.out = src, recv, out
-        self.time = self.cost(size_of(src))
+        self.cost(size_of(src), 4)
 
     def start(self):
         for d, to in enumerate(self.others()):
@@ -351,7 +379,7 @@
     def __init__(self, wires, axis, full):
         super().__init__(wires, axis)
         self.full = full
-        self.time = self.cost(size_of(full) // full.shape[0])
+        self.cost(size_of(full) // full.shape[0])
 
     def start(self):
         own = self.full.at[self.wires.at[self.axis]]
@@ -365,7 +393,6 @@
 class Plane(Step):
     def __init__(self, wires, axes):
         super().__init__(wires, axes)
-        self.hop = HOP + 1.0
 
     def here(self):
         return tuple(self.wires.at[axis] for axis in self.axis)
@@ -389,7 +416,7 @@
     def __init__(self, wires, axes, src, recv, out):
         super().__init__(wires, axes)
         self.src, self.recv, self.out = src, recv, out
-        self.time = self.hop + size_of(out) * 8 / LINK
+        self.cost(size_of(out), 16)
 
     def start(self):
         for d, to in enumerate(self.others()):
@@ -409,7 +436,7 @@
     def __init__(self, wires, axes, full):
         super().__init__(wires, axes)
         self.full = full
-        self.time = self.hop + size_of(full) / 16 * 8 / LINK
+        self.cost(size_of(full) // 16)
 
     def start(self):
         own = self.full.at[self.here()]
@@ -432,7 +459,8 @@
     def __init__(self, wires, axis, src, recv, out):
         super().__init__(wires, axis)
         self.src, self.recv, self.out = src, recv, out
-        self.time = HOP + size_of(out) / 2 / LINK
+        self.load = {axis: size_of(out) / 2 / LINK}
+        self.work = size_of(out) / 2 * 3 * ADD
 
     def start(self):
         own, near, back, far = ring(self.wires.at, self.axis)
@@ -457,7 +485,8 @@
     def __init__(self, wires, axis, src, recv, out):
         super().__init__(wires, axis)
         self.src, self.recv, self.out = src, recv, out
-        self.time = HOP + size_of(out) / 2 / LINK
+        self.load = {axis: size_of(out) / 2 / LINK}
+        self.work = size_of(out) / 2 * 3 * ADD
 
     def start(self):
         own, near, back, far = ring(self.wires.at, self.axis)
@@ -470,9 +499,42 @@
             add_into(self.out, (HALVES[half],), [self.src.at[half, 0], self.recv.at[half]])
 
 
+class UnfoldFirst(Step):
+    def __init__(self, wires, axis, full):
+        super().__init__(wires, axis)
+        self.full = full
+        self.load = {axis: size_of(full) / 8 / LINK}
+
+    def start(self):
+        own, near, back, far = ring(self.wires.at, self.axis)
+        for half, to in ((0, near), (1, back)):
+            block = self.full.at[own, HALVES[half]]
+            self.send(block, block, to)
+
+    def finish(self):
+        self.wait()
+
+
+class UnfoldSecond(Step):
+    def __init__(self, wires, axis, full):
+        super().__init__(wires, axis)
+        self.full = full
+        self.load = {axis: size_of(full) / 4 / LINK}
+
+    def start(self):
+        own, near, back, far = ring(self.wires.at, self.axis)
+        for half, other, to in ((0, near, back), (1, back, near)):
+            for index in (own, other):
+                block = self.full.at[index, HALVES[half]]
+                self.send(block, block, to)
+
+    def finish(self):
+        self.wait()
+
+
 class Chain:
     def __init__(self, steps):
-        self.steps, self.next = steps, 0
+        self.steps, self.next, self.after = steps, 0, None
 
     def advance(self):
         if self.next > 0:
@@ -484,19 +546,34 @@
 
 class Clock:
     def __init__(self):
-        self.now, self.active = 0.0, []
+        self.now, self.active, self.busy = 0.0, [], {}
+
+    def started(self, chain):
+        step = chain.steps[chain.next - 1]
+        ends = [self.now]
+        for axis, load in step.load.items():
+            self.busy[axis] = max(self.now, self.busy.get(axis, 0.0)) + load
+            ends.append(self.busy[axis])
+        chain.due = max(ends) + step.hop
 
     def begin(self, chain):
-        chain.advance()
-        chain.due = self.now + chain.steps[0].time
+        chain.steps[0].start()
+        self.begun(chain)
+
+    def begun(self, chain):
+        chain.next = 1
+        self.started(chain)
         self.active.append(chain)
 
     def step(self, chain):
+        self.now += chain.steps[chain.next - 1].work
         chain.advance()
         if chain.next > len(chain.steps):
             self.active.remove(chain)
+            if chain.after is not None:
+                chain.after()
         else:
-            chain.due = max(self.now, chain.due) + chain.steps[chain.next - 1].time
+            self.started(chain)
 
     def passed(self, time):
         self.now += time
@@ -511,33 +588,77 @@
             self.step(chain)
 
 
-def spread_steps(wires, axes, src, recvs, sums, last):
-    first, second, third = axes
-    return [
-        Scatter(wires, "core", src, recvs[0], sums[0]),
-        FoldFirst(wires, first, sums[0], recvs[1], sums[1]),
-        FoldSecond(wires, first, sums[1], recvs[2], sums[2]),
-        Scatter(wires, second, sums[2], recvs[3], sums[3]),
-        Scatter(wires, third, sums[3], recvs[4], last),
-    ]
-
-
-def whole_chain(wires, axes, src, recvs, sums, full):
+class Group(Step):
+    def __init__(self, steps):
+        self.steps = steps
+        self.hop, self.work = max(step.hop for step in steps), sum(step.work for step in steps)
+        axes = {axis for step in steps for axis in step.load}
+        self.load = {axis: sum(step.load.get(axis, 0.0) for step in steps) for axis in axes}
+
+    def start(self):
+        for step in self.steps:
+            step.start()
+
+    def finish(self):
+        for step in self.steps:
+            step.finish()
+
+
+def scatter_scratch(plan, width):
+    block = (16, width)
+    recvs, sums, left = [pltpu.VMEM((1, 4, 4, 4, *block), BF16)], [pltpu.VMEM((4, 4, 4, *block), BF16)], 3
+    for kind, _ in plan:
+        if kind == "fold":
+            rest = (4,) * (left - 2) + block
+            recvs += [pltpu.VMEM((2, 2, 2, *rest), BF16), pltpu.VMEM((2, 2, *rest), BF16)]
+            sums += [pltpu.VMEM((2, 2, 2, *rest), BF16), pltpu.VMEM((4, *rest), BF16)]
+            left -= 1
+        else:
+            left -= 2 if kind == "plane" else 1
+            rest = (4,) * left + block
+            recvs.append(pltpu.VMEM((15 if kind == "plane" else 3, *rest), BF16))
+            sums.append(pltpu.VMEM(rest, BF16))
+    return recvs, sums[:-1]
+
+
+def scatter_steps(wires, plan, src, recvs, sums, last):
+    outs = [*sums, last]
+    steps = [Scatter(wires, "core", src, recvs[0], outs[0])]
+    for kind, axes in plan:
+        kinds = {"fold": [FoldFirst, FoldSecond], "plane": [PlaneScatter], "axis": [Scatter]}[kind]
+        for form in kinds:
+            k = len(steps)
+            steps.append(form(wires, axes, outs[k - 1], recvs[k], outs[k]))
+    return steps
+
+
+def plan_axes(plan):
+    return [axis for kind, axes in plan for axis in (axes if kind == "plane" else (axes,))]
+
+
+def whole_steps(wires, plan, src, recvs, sums, full):
     at = wires.at
-    core, first, second, third = at["core"], *(at[axis] for axis in axes)
-    return Chain([
-        Scatter(wires, "core", src, recvs[0], sums[0]),
-        PlaneScatter(wires, axes[:2], sums[0], recvs[1], sums[1]),
-        Scatter(wires, axes[2], sums[1], recvs[2], full.at[core, first, second, third]),
-        Gather(wires, axes[2], full.at[core, first, second]),
-        PlaneGather(wires, axes[:2], full.at[core]),
-        Gather(wires, "core", full),
-    ])
-
-
-def part_chain(wires, axes, src, recvs, sums, full):
-    steps = spread_steps(wires, axes, src, recvs, sums, full.at[wires.at["var"]])
-    return Chain(steps + [Gather(wires, "var", full)])
+    where = [at["core"], *(at[axis] for axis in plan_axes(plan))]
+    steps = scatter_steps(wires, plan, src, recvs, sums, full.at[tuple(where)])
+    for kind, axes in reversed(plan):
+        where = where[: len(where) - (2 if kind == "plane" else 1)]
+        part = full.at[tuple(where)]
+        if kind == "plane":
+            steps.append(PlaneGather(wires, axes, part))
+        elif kind == "fold":
+            steps += [UnfoldFirst(wires, axes, part), UnfoldSecond(wires, axes, part)]
+        else:
+            steps.append(Gather(wires, axes, part))
+    return steps + [Gather(wires, "core", full)]
+
+
+def part_steps(wires, plan, src, recvs, sums, full):
+    last = full.at[wires.at["var"]]
+    return scatter_steps(wires, plan, src, recvs, sums, last) + [Gather(wires, "var", full)]
+
+
+def lock_step(*lists):
+    return Chain([Group(steps) for steps in zip(*lists)])
 
 
 def small_chain(wires, src, recvs, sums, full):
@@ -551,35 +672,6 @@
     ])
 
 
-def chain_scratch(width):
-    block = (16, width)
-    recvs = [
-        pltpu.VMEM((1, 4, 4, 4, *block), BF16),
-        pltpu.VMEM((2, 2, 2, 4, *block), BF16),
-        pltpu.VMEM((2, 2, 4, *block), BF16),
-        pltpu.VMEM((3, 4, *block), BF16),
-        pltpu.VMEM((3, *block), BF16),
-    ]
-    sums = [
-        pltpu.VMEM((4, 4, 4, *block), BF16),
-        pltpu.VMEM((2, 2, 2, 4, *block), BF16),
-        pltpu.VMEM((4, 4, *block), BF16),
-        pltpu.VMEM((4, *block), BF16),
-    ]
-    return recvs, sums
-
-
-def whole_scratch(width):
-    block = (16, width)
-    recvs = [
-        pltpu.VMEM((1, 4, 4, 4, *block), BF16),
-        pltpu.VMEM((15, 4, *block), BF16),
-        pltpu.VMEM((3, *block), BF16),
-    ]
-    sums = [pltpu.VMEM((4, 4, 4, *block), BF16), pltpu.VMEM((4, *block), BF16)]
-    return recvs, sums
-
-
 SMALL_SHAPE = (2, 4, 4, 16, TILE)
 
 
@@ -599,26 +691,29 @@
 
 
 WEIGHTS = 10
+UP_PLAN = (("fold", "x"), ("axis", "z"), ("axis", "y"))
+DOWN_PLAN = (("fold", "y"), ("axis", "z"), ("axis", "x"))
+OUT_PLAN = (("axis", "z"), ("plane", ("x", "y")))
+VALUE_PLAN = (("plane", ("x", "y")), ("axis", "z"))
 
 
 def main_kernel(
     pixels, w_embed_h, level_embed_h, latents_h, w_query_h, w_key_h, w_value_h, w_out_h, w_up_h, w_down_h, cot_h,
-    pooled, up_all, down_all, out_all, value_all, small_all,
+    pooled, up_all, down_all, out_all, value_all, small_all, rows, d_queries, d_lat,
     loaded, work, grads, scratch, load_sem, send_sem, recv_sem,
 ):
     w_embed, level_embed, latents, w_query, w_key, w_value, w_out, w_up, w_down, cot, px = loaded
     (
         select, wq_high, wq_low, level_rows, unit, inv, normed, normed_t, values, scores, weights, spread, mixed,
-        attended, pool_sum, d_att, d_att_b, d_mixed, d_values, d_weights, d_scores, hidden, d_pre, small, rest,
+        attended, d_att, d_att_b, d_mixed, d_values, d_weights, d_scores, hidden, d_pre, d_hidden, small, rest,
     ) = work
     up, down, out, value, small_b = grads
     at = place()
     wires = Wires(at, send_sem, recv_sem)
 
     pairs = [
-        (latents_h, latents), (w_query_h, w_query), (w_key_h, w_key), (w_embed_h, w_embed),
-        (level_embed_h, level_embed), (w_value_h, w_value), (w_out_h, w_out), (cot_h, cot),
-        (w_up_h, w_up), (w_down_h, w_down),
+        (latents_h, latents), (w_query_h, w_query), (w_key_h, w_key), (cot_h, cot), (w_down_h, w_down),
+        (w_embed_h, w_embed), (level_embed_h, level_embed), (w_value_h, w_value), (w_out_h, w_out), (w_up_h, w_up),
     ]
     loads = [pltpu.make_async_copy(src, dst, load_sem.at[i]) for i, (src, dst) in enumerate(pairs)]
     for load in loads:
@@ -639,8 +734,16 @@
 
     for load in loads[:3]:
         load.wait()
-    prepare(latents, w_query, w_key, select, wq_high, wq_low)
-    for load in loads[3:6]:
+    prepare(latents, w_query, w_key, select, wq_high, wq_low, rows)
+    for load in loads[3:5]:
+        load.wait()
+
+    @pl.loop(0, w_down.shape[0] // TILE, unroll=2)
+    def _(t):
+        cols = pl.ds(pl.multiple_of(t * TILE, TILE), TILE)
+        d_hidden[:, cols] = mm_nt(cot[...], w_down[cols, :])
+
+    for load in loads[5:8]:
         load.wait()
     keep.wait()
     for move in moves:
@@ -650,54 +753,54 @@
     )
     softmax(scores, weights)
     mix(weights, select, values, spread, mixed)
-    for load in loads[6:]:
+    for load in loads[8:]:
         load.wait()
     attend(latents, mixed, w_out, attended)
 
-    chain_down = part_chain(wires, ("z", "x", "y"), down, *scratch[0], down_all)
-    chain_up = part_chain(wires, ("x", "z", "y"), up, *scratch[1], up_all)
-    chain_out = whole_chain(wires, ("x", "y", "z"), out, *scratch[2], out_all)
-    chain_value = whole_chain(wires, ("y", "z", "x"), value, *scratch[3], value_all)
+    chain_ffn = lock_step(
+        part_steps(wires, DOWN_PLAN, down, *scratch[0], down_all),
+        part_steps(wires, UP_PLAN, up, *scratch[1], up_all),
+    )
+    chain_att = lock_step(
+        whole_steps(wires, OUT_PLAN, out, *scratch[2], out_all),
+        whole_steps(wires, VALUE_PLAN, value, *scratch[3], value_all),
+    )
     chain_small = small_chain(wires, small_b, *scratch[4], small_all)
     clock = Clock()
 
-    feed_forward(attended, cot, w_up, w_down, pool_sum, d_att, hidden, d_pre)
+    feed_forward(attended, cot, w_up, d_hidden, d_att, hidden, d_pre)
     d_att_b[...] = d_att[...].astype(BF16)
+    first = chain_att.steps[0]
     for half in range(2):
         block = mm_tn(mixed[...], d_att_b[:, half * TILE : (half + 1) * TILE]).astype(BF16)
         out[half] = block.reshape(4, 4, 4, 16, TILE)
-    clock.begin(chain_out)
+    first.steps[0].start()
     d_mixed[...] = mm_nt(d_att_b[...], w_out[...]).astype(BF16)
-    clock.passed(0.8)
     for t in range(4):
         block = value_grad(t, spread, d_mixed, normed_t, d_values)
         value[t // 2, t % 2 * 2 : t % 2 * 2 + 2] = block.reshape(2, 4, 4, 16, TILE)
-        clock.passed(0.7)
-    clock.begin(chain_value)
-
+    first.steps[1].start()
+    clock.begun(chain_att)
     for t in range(8):
         cols = slice(t * TILE, (t + 1) * TILE)
+        x, z_hi = t // 2, t % 2
         block = mm_tn(hidden[:, cols], cot[...]).astype(BF16)
+        other = mm_tn(d_pre[:, cols], attended[...]).astype(BF16)
         for core in range(2):
             for var in range(8):
+                z, y = z_hi * 2 + var // 4, var % 4
                 start = core * 128 + var * 16
-                down[core, t % 2 * 2 + var // 4, t // 2, var % 4] = block[start : start + 16]
-        clock.passed(0.25)
-    clock.begin(chain_down)
-    for t in range(8):
-        cols = slice(t * TILE, (t + 1) * TILE)
-        block = mm_tn(d_pre[:, cols], attended[...]).astype(BF16)
-        for core in range(2):
-            for var in range(8):
-                start = core * 128 + var * 16
-                up[core, t // 2, t % 2 * 2 + var // 4, var % 4] = block[start : start + 16]
-        clock.passed(0.25)
-    clock.begin(chain_up)
-
+                down[core, y, z, x] = block[start : start + 16]
+                up[core, x, z, y] = other[start : start + 16]
+        clock.passed(0.5)
+    clock.begin(chain_ffn)
+    for q in range(LAT):
+        rows = slice(q * ROWS, (q + 1) * ROWS)
+        pooled[rows, :] = (attended[rows, :].astype(F32) + mm(hidden[rows, :], w_down[...])).astype(BF16)
+    clock.passed(1.0)
     weight_grad(d_mixed, values, select, d_weights)
     clock.passed(2.5)
     score_back(scores, d_weights, d_scores)
-    pooled[...] = pool_sum[...].astype(BF16)
     clock.passed(0.5)
     small[...] = jnp.zeros_like(small)
     rest[...] = jnp.zeros_like(rest)
@@ -713,6 +816,7 @@
         small_b[0, 2 * k : 2 * k + 2] = small[:, cols].astype(BF16).reshape(2, 4, 16, TILE)
         small_b[1, 0, k] = rest[:, cols].astype(BF16)
     clock.passed(0.5)
+    chain_small.after = lambda: query_back(small_all, w_query, w_key, d_queries, d_lat)
     clock.begin(chain_small)
     clock.drain()
 
@@ -741,7 +845,6 @@
         vmem((pairs, inner), BF16),
         vmem((pairs, width), BF16),
         vmem((pairs, width), F32),
-        vmem((pairs, width), F32),
         vmem((pairs, width), BF16),
         vmem((pairs, inner), BF16),
         vmem((every, inner), BF16),
@@ -749,6 +852,7 @@
         vmem((every, PAD), BF16),
         vmem((pairs, w_up.shape[1]), BF16),
         vmem((pairs, w_up.shape[1]), BF16),
+        vmem((pairs, w_up.shape[1]), F32),
         vmem((128, width), F32),
         vmem((16, width), F32),
     ]
@@ -768,14 +872,23 @@
             shape(chain_shapes(TILE), BF16),
             shape(chain_shapes(TILE), BF16),
             shape(SMALL_SHAPE, BF16),
+            shape((48, inner), BF16),
+            shape((8, inner), F32),
+            shape((8, width), F32),
         ),
         in_specs=[pl.BlockSpec(memory_space=pl.ANY)] * 11,
-        out_specs=(whole,) * 6,
+        out_specs=(whole,) * 9,
         scratch_shapes=[
             loaded,
             work,
             grads,
-            [chain_scratch(width), chain_scratch(width), whole_scratch(TILE), whole_scratch(TILE), small_scratch()],
+            [
+                scatter_scratch(DOWN_PLAN, width),
+                scatter_scratch(UP_PLAN, width),
+                scatter_scratch(OUT_PLAN, TILE),
+                scatter_scratch(VALUE_PLAN, TILE),
+                small_scratch(),
+            ],
             pltpu.SemaphoreType.DMA((WEIGHTS + 1,)),
             pltpu.SemaphoreType.DMA((SEMS,)),
             pltpu.SemaphoreType.DMA((SEMS,)),
@@ -788,13 +901,13 @@
 
 
 def finish_kernel(
-    small_h, value_h, out_h, up_h, down_h, latents, w_query_h, w_key_h,
-    grad_embed, grad_level, grad_lat, grad_up, grad_down, query_h, key_h, value_g, out_g,
-    small, value_all, out_all, w_query, w_key, grad_query, grad_key, grad_value, grad_out, up_part, down_part,
-    load_sem, save_sem,
+    small_h, rows_h, queries_h, value_h, out_h, up_h, down_h, pooled_h, d_lat, latents,
+    grad_embed, grad_level, grad_lat, grad_up, grad_down, query_h, key_h, value_g, out_g, pooled_g,
+    small, rows, d_queries, value_all, out_all, up_part, down_part,
+    grad_query, grad_key, grad_value, grad_out, load_sem, save_sem,
 ):
     pairs = [
-        (value_h, value_all), (out_h, out_all), (small_h, small), (w_query_h, w_query), (w_key_h, w_key),
+        (small_h, small), (rows_h, rows), (queries_h, d_queries), (value_h, value_all), (out_h, out_all),
         (up_h, up_part), (down_h, down_part),
     ]
     loads = [pltpu.make_async_copy(src, dst, load_sem.at[i]) for i, (src, dst) in enumerate(pairs)]
@@ -807,41 +920,34 @@
         copy.start()
         saves.append(copy)
 
-    width, inner = w_key.shape
-    loads[0].wait()
+    width, inner = grad_key.shape
+    save(pooled_h, pooled_g)
+    for load in loads[0:3]:
+        load.wait()
+    sums = jnp.concatenate([small[0, 2 * k : 2 * k + 2].reshape(128, TILE) for k in range(2)], axis=1)
+    rest = jnp.concatenate([small[1, 0, k] for k in range(2)], axis=1)
+    total = sums[0:48, :]
+    for t in range(2):
+        cols = slice(t * 512, (t + 1) * 512)
+        grad_key[:, cols] = mm_tn(total, rows[:, cols])
+        save(grad_key.at[:, cols], key_h.at[:, cols])
+    high, low = split(d_queries[0:LAT, :])
+    for t in range(2):
+        cols = slice(t * 512, (t + 1) * 512)
+        grad_query[:, cols] = mm_tn(latents[...], high[:, cols]) + mm_tn(latents[...], low[:, cols])
+        save(grad_query.at[:, cols], query_h.at[:, cols])
+    loads[3].wait()
     for t in range(4):
         block = value_all[t // 2, t % 2 * 2 : t % 2 * 2 + 2].reshape(width, TILE)
         cols = slice(t * TILE, (t + 1) * TILE)
         grad_value[:, cols] = block.astype(F32)
         save(grad_value.at[:, cols], value_g.at[:, cols])
-    loads[1].wait()
+    loads[4].wait()
     for half in range(2):
         cols = slice(half * TILE, (half + 1) * TILE)
         grad_out[:, cols] = out_all[half].reshape(inner, TILE).astype(F32)
         save(grad_out.at[:, cols], out_g.at[:, cols])
-    for load in loads[2:5]:
-        load.wait()
-    sums = jnp.concatenate([small[0, 2 * k : 2 * k + 2].reshape(128, TILE) for k in range(2)], axis=1)
-    rest = jnp.concatenate([small[1, 0, k] for k in range(2)], axis=1)
-    total = sums[0:48, :]
-    rows = query_rows(latents[...], w_query[...])
-    for t in range(2):
-        cols = slice(t * 512, (t + 1) * 512)
-        grad_key[:, cols] = mm_tn(total, rows[0:48, cols])
-        save(grad_key.at[:, cols], key_h.at[:, cols])
-    spread = mm(total, w_key[...])
-    row = lax.broadcasted_iota(jnp.int32, (48, inner), 0)
-    head = lax.broadcasted_iota(jnp.int32, (48, inner), 1) // HEAD
-    own = []
-    for q in range(LAT):
-        own.append(jnp.sum(jnp.where(row == q * HEADS + head, spread, 0.0), axis=0, keepdims=True))
-    d_queries = jnp.concatenate(own, axis=0)
-    high, low = split(d_queries)
-    for t in range(2):
-        cols = slice(t * 512, (t + 1) * 512)
-        grad_query[:, cols] = mm_tn(latents[...], high[:, cols]) + mm_tn(latents[...], low[:, cols])
-        save(grad_query.at[:, cols], query_h.at[:, cols])
-    grad_lat[...] = rest[8:11, :].astype(F32) + mm_nt(high, w_query[...]) + mm_nt(low, w_query[...])
+    grad_lat[...] = d_lat[0:LAT, :]
     grad_embed[...] = sums[48:128, :].astype(F32)
     grad_level[...] = rest[0:8, :].astype(F32)
     for load in loads[5:]:
@@ -852,13 +958,14 @@
         copy.wait()
 
 
-def finish(small, value_all, out_all, up_part, down_part, latents, w_query, w_key):
-    width, inner = w_key.shape
+def finish(small, rows, d_queries, value_all, out_all, up_part, down_part, pooled, d_lat, latents):
+    width, inner = latents.shape[1], rows.shape[1]
     shape = jax.ShapeDtypeStruct
     whole = pl.BlockSpec(memory_space=pltpu.VMEM)
     anywhere = pl.BlockSpec(memory_space=pl.ANY)
     vmem = pltpu.VMEM
-    embed, level, lat, up, down, query, key, value, out = pl.pallas_call(
+    loaded = (small, rows, d_queries, value_all, out_all, up_part, down_part)
+    embed, level, lat, up, down, query, key, value, out, pooled = pl.pallas_call(
         finish_kernel,
         out_shape=(
             shape((80, width), F32),
@@ -870,39 +977,36 @@
             shape((width, inner), F32),
             shape((width, inner), F32),
             shape((inner, width), F32),
+            shape(pooled.shape, BF16),
         ),
-        in_specs=[anywhere] * 5 + [whole] + [anywhere] * 2,
-        out_specs=(whole,) * 5 + (anywhere,) * 4,
-        scratch_shapes=[
-            vmem(small.shape, BF16),
-            vmem(value_all.shape, BF16),
-            vmem(out_all.shape, BF16),
-            vmem(w_query.shape, BF16),
-            vmem(w_key.shape, BF16),
+        in_specs=[anywhere] * 8 + [whole] * 2,
+        out_specs=(whole,) * 5 + (anywhere,) * 5,
+        scratch_shapes=[vmem(array.shape, array.dtype) for array in loaded]
+        + [
             vmem((width, inner), F32),
             vmem((width, inner), F32),
             vmem((width, inner), F32),
             vmem((inner, width), F32),
-            vmem(up_part.shape, BF16),
-            vmem(down_part.shape, BF16),
             pltpu.SemaphoreType.DMA((7,)),
-            pltpu.SemaphoreType.DMA((10,)),
+            pltpu.SemaphoreType.DMA((11,)),
         ],
         compiler_params=pltpu.CompilerParams(vmem_limit_bytes=60 * 1024 * 1024),
         name="finish",
-    )(small, value_all, out_all, up_part, down_part, latents, w_query, w_key)
-    return embed, level, lat, query, key, value, out, up, down
+    )(*loaded, pooled, d_lat, latents)
+    return pooled, embed, level, lat, query, key, value, out, up, down
 
 
 def on_device(
     pixels, w_embed, level_embed, latents, w_query, w_key, w_value, w_out, w_up, w_down, cotangent
 ):
     width = w_embed.shape[1]
-    pooled, up_part, down_part, out_all, value_all, small = main_part(
+    pooled, up_part, down_part, out_all, value_all, small, rows, d_queries, d_lat = main_part(
         pixels[0], w_embed, level_embed, latents, w_query, w_key, w_value, w_out, w_up, w_down,
         cotangent.reshape(LAT * ROWS, width),
     )
-    grads = finish(small, value_all, out_all, up_part, down_part, latents, w_query, w_key)
+    pooled, *grads = finish(
+        small, rows, d_queries, value_all, out_all, up_part, down_part, pooled, d_lat, latents
+    )
     return (pooled.reshape(LAT, ROWS, width), *grads)
 
 

time: 96.6 us -> 90.4 us (0.936)
  Pallas kernels: 95 us -> 89.3 us
    pallas_call x1, Pallas kernels: 88.5 us -> 74.6 us  [main_part(): pl.pallas_call(main_kernel, out_shape=(shape((pairs, width), BF16), shape...]
    pallas_call x1, Pallas kernels: 6.54 us -> 14.8 us  [finish(): pl.pallas_call(finish_kernel, out_shape=(shape((80, width), F32), shape((...]
where the time goes in v4:
time: 90.4 us; the launch traced here: 90.2 us
  Pallas kernels  89.3 us (99%)
    pallas_call x1, Pallas kernels, main_part(): pl.pallas_call(main_kernel, out_shape=(shape((pairs, width), BF16), shape...  74.6 us
    pallas_call x1, Pallas kernels, finish(): pl.pallas_call(finish_kernel, out_shape=(shape((80, width), F32), shape((...  14.8 us

profile of v4, /device:TPU:0, one launch (start us, length us, event | category | flops | bytes accessed | tf_op | source)
XLA Modules:
  0.0 90.2 jit_solution(16527597189933466807)
XLA Ops:
  0.6 74.6 %main_part.1 = (bf16[384,512]{1,0:T(8,128)(2,1)}, bf16[8,16,512]{2,1,0:T(8,128)(2,1)}, bf16[8,16,512]{2,1,0:T(8,128)(2,1)}, bf16[2,4,4,4,16,256]{5,4,3,2,1,0:T(8...) custom-call(bf16[5,16,1024]{2,1,0:T(8,128)(2,1)} %bitcast.4, ...), custom_call_target="tpu_custom_call" | custom-call | tf_op jit(solution)/shard_map/main_part/pallas_call | solution.py:866
  75.2 14.8 %finish.1 = (f32[80,512]{1,0:T(8,128)}, f32[8,512]{1,0:T(8,128)}, f32[3,512]{1,0:T(4,128)}, f32[512,128]{1,0:T(8,128)}, f32[128,512]{1,0:T(8,128)}, /*index=5*/f...) custom-call(bf16[2,4,4,16,256]{4,3,2,1,0:T(8,128)(2,1)} %get-tuple-e, ...), custom_call_target="tpu_custom_call" | custom-call | tf_op jit(solution)/shard_map/finish/pallas_call | solution.py:968
